TPU v7x, 32 devices: a whole 2x2x4 slice. The times are simulated.
32 devices in a mesh: items: 8 (over y, x, core), frames: 4 (over z).
Axes of the slice: x: 2, y: 2, z: 4, core: 2. Of those that a mesh axis runs over, the one named last changes fastest.
Arguments:
- media: bfloat16 [32, 4, 256, 1536], P('items', 'frames'), may hold values from -6 to 6
- cotangent: float32 [32, 64, 1536], P('items', 'frames'), may hold values from -6 to 6
- frame_count: int32 [32], replicated, may hold values from 1 to 4, as said below
- frame_start: int32 [32], replicated, may hold values from 0 to 3
- latents: float32 [64, 1536], replicated, may hold values from -6 to 6
- time_embed: float32 [4, 1536], replicated, may hold values from -6 to 6
- media_gain: float32 [1536], replicated, may hold values from 0.5 to 1.5
- media_bias: float32 [1536], replicated, may hold values from -4 to 4
- latent_gain: float32 [1536], replicated, may hold values from 0.5 to 1.5
- latent_bias: float32 [1536], replicated, may hold values from -4 to 4
- ffn_gain: float32 [1536], replicated, may hold values from 0.5 to 1.5
- ffn_bias: float32 [1536], replicated, may hold values from -4 to 4
- query_weight: bfloat16 [1536, 1536], P('items'), may hold values from -0.21875 to 0.21875
- key_weight: bfloat16 [1536, 1536], P('items'), may hold values from -0.21875 to 0.21875
- value_weight: bfloat16 [1536, 1536], P('items'), may hold values from -0.15625 to 0.15625
- out_weight: bfloat16 [1536, 1536], P('items'), may hold values from -0.875 to 0.875
- up_weight: bfloat16 [1536, 6144], P('items'), may hold values from -0.15625 to 0.15625
- down_weight: bfloat16 [6144, 1536], P('items'), may hold values from -0.078125 to 0.078125
Outputs:
- latents_out: float32 [32, 64, 1536], P('items', 'frames')
- entropy: float32 [32, 64], P('items', 'frames')
- media_grad: bfloat16 [32, 4, 256, 1536], P('items', 'frames')
- latents_grad: float32 [64, 1536], replicated
- time_grad: float32 [4, 1536], P(None, 'items')
- media_gain_grad: float32 [1536], P('items')
- media_bias_grad: float32 [1536], P('items')
- latent_gain_grad: float32 [1536], replicated
- latent_bias_grad: float32 [1536], replicated
- ffn_gain_grad: float32 [1536], replicated
- ffn_bias_grad: float32 [1536], replicated
- query_grad: float32 [1536, 1536], P('items')
- key_grad: float32 [1536, 1536], P('items')
- value_grad: float32 [1536, 1536], P('items')
- out_grad: float32 [1536, 1536], P('items')
- up_grad: float32 [1536, 6144], P('items')
- down_grad: float32 [6144, 1536], P('items')
Inputs may be any that keep to these rules, and one draw needn't show every extreme that they name: `frame_count`: items whose index is 0 or 1 modulo 4 are single images with one frame; the others are clips of 2 to 4 frames, and each aligned block of 4 items holds a clip of all 4 frames.
All inputs are finite; a program needn't handle non-finite values.
Results may differ from a plain program's by a relative error of at most 0.0128.
The roundings to bfloat16 on the way count: a program that leaves them out, or rounds other values in their place, can miss the bound.
Values may be sent and summed in bfloat16 or wider, within the bound.
No kernel may reach another device: no remote copies, remote signals or barrier semaphores. Data moves between devices by JAX's collectives and lax.ppermute only.
A program may use at most 320 MiB of HBM per device.

v0:
```python
import functools
import math

import jax
import jax.numpy as jnp
from jax import lax
from jax.experimental import pallas as pl
from jax.experimental.pallas import tpu as pltpu
from jax.sharding import PartitionSpec as P

HEADS = 16
GROUP = 4
CHUNKS = 2
LANES = 128
EPSILON = 1e-05
MASKED = -1e30
F32 = jnp.float32
BF16 = jnp.bfloat16
HIGHEST = lax.Precision.HIGHEST


def layer_norm(inputs, norm_gain, norm_bias):
    center = inputs - jnp.mean(inputs, axis=-1, keepdims=True)
    spread = jnp.mean(center * center, axis=-1, keepdims=True)
    return center * lax.rsqrt(spread + EPSILON) * norm_gain + norm_bias


def matmul(left_side, right_side):
    return jnp.dot(left_side, right_side, preferred_element_type=F32)


def transposed_left(left_side, right_side):
    return lax.dot_general(
        left_side, right_side, (((0,), (0,)), ((), ())), preferred_element_type=F32
    )


def transposed_right(left_side, right_side):
    return lax.dot_general(
        left_side, right_side, (((1,), (1,)), ((), ())), preferred_element_type=F32
    )


def send_on(x, axis, step):
    size = lax.axis_size(axis)
    return lax.ppermute(x, axis, [(i, (i + step) % size) for i in range(size)])


def send_across(x, axis, distance):
    return lax.ppermute(x, axis, [(i, i ^ distance) for i in range(lax.axis_size(axis))])


def spread_on(x, axis):
    return [x] + [send_on(x, axis, s) for s in range(1, lax.axis_size(axis))]


def spread_across(x, axis):
    chips = [x] + [send_across(x, axis, d) for d in range(2, lax.axis_size(axis), 2)]
    return [b for block in chips for b in (block, send_across(block, axis, 1))]


def collect_across(pieces, axis):
    return [pieces[0]] + [send_across(p, axis, d) for d, p in enumerate(pieces) if d]


def total_of(pieces):
    return functools.reduce(jnp.add, [p.astype(F32) for p in pieces])


def after(x, *earlier):
    return lax.optimization_barrier((x,) + earlier)[0]


def split_terms(x):
    high = x.astype(BF16)
    rest = x - high.astype(F32)
    middle = rest.astype(BF16)
    return high, middle, (rest - middle.astype(F32)).astype(BF16)


def iota(shape, dim):
    return lax.broadcasted_iota(jnp.int32, shape, dim)


def head_masks(rows, width, head_size):
    lane = iota((rows, width), 1)
    return [
        jnp.logical_and(lane >= h * head_size, lane < (h + 1) * head_size)
        for h in range(width // head_size)
    ]


def spread_heads(block, masks):
    return jnp.concatenate([jnp.where(m, block, jnp.zeros_like(block)) for m in masks], 0)


def collect_heads(block, masks):
    rows = block.shape[0] // len(masks)
    total = jnp.where(masks[0], block[:rows], 0.0)
    for h in range(1, len(masks)):
        total = total + jnp.where(masks[h], block[h * rows : (h + 1) * rows], 0.0)
    return total


def head_expand(width, head_size):
    row, column = iota((LANES, width), 0), iota((LANES, width), 1)
    return jnp.logical_and(column >= row * head_size, column < (row + 1) * head_size).astype(F32)


def live_rows(flag_ref, item, items, patches, lats, columns):
    row = iota((patches + lats, columns), 0)
    media = jnp.logical_and(row < patches, flag_ref[item] > 0)
    return jnp.logical_or(media, jnp.logical_and(row >= patches, flag_ref[items] > 0))


def pack_shape(own, shard, width):
    unit = math.gcd(own, shard)
    return unit, width * unit // shard


def join_kernel(key_ref, value_ref, cotangent_ref, out_ref, low_ref, *, width):
    for g in range(key_ref.shape[1] // width):
        columns = slice(g * width, (g + 1) * width)
        out_ref[:, 2 * g * width : (2 * g + 1) * width] = key_ref[:, columns]
        out_ref[:, (2 * g + 1) * width : (2 * g + 2) * width] = value_ref[:, columns]
    low = cotangent_ref[...].astype(BF16)
    low_ref[...] = low
    own, span = low.shape
    unit, piece = pack_shape(own, out_ref.shape[0], span)
    for a in range(own // unit):
        for b in range(span // piece):
            at = 2 * span + a * piece
            out_ref[b * unit : (b + 1) * unit, at : at + piece] = low[
                a * unit : (a + 1) * unit, b * piece : (b + 1) * piece
            ]


def norm_kernel(media_ref, time_ref, gain_ref, bias_ref, lat_ref, out_ref, *, steps, per_item):
    step = pl.program_id(0)

    @pl.when(step < steps)
    def _():
        rows = media_ref[...].astype(F32) + time_ref[pl.ds(step // per_item, 1), :]
        out_ref[...] = layer_norm(rows, gain_ref[...], bias_ref[...]).astype(BF16)

    @pl.when(step == steps)
    def _():
        out_ref[...] = lat_ref[...]


def forward_kernel(
    flag_ref, both_ref, query_ref, top_ref, *refs, items, patches, scale, head_size, heads,
):
    message_refs, (part_ref, mark_ref) = refs[:-2], refs[-2:]
    lats, width = query_ref.shape
    frames = len(message_refs)
    own = message_refs[0].shape[0]
    row_total = own // items
    masks = head_masks(lats, width, head_size)
    queries = spread_heads(query_ref[...].astype(F32), masks).astype(BF16)
    base = items * patches
    lat_both = both_ref[base : base + lats, :]
    group = pl.program_id(0)
    term, lane = iota((16, GROUP * LANES), 0), iota((16, GROUP * LANES), 1)
    place = jnp.logical_and(
        lane % LANES == term * heads + group * GROUP + lane // LANES, term < 9
    ).astype(BF16)
    for i in range(items):
        both = jnp.concatenate([both_ref[i * patches : (i + 1) * patches, :], lat_both], 0)
        live = live_rows(flag_ref, i, items, patches, lats, queries.shape[0])
        scores = scale * transposed_right(both[:, :width], queries)
        masked = jnp.where(live, scores, MASKED)
        top = jnp.max(masked, axis=0, keepdims=True)
        block_exp = jnp.where(live, jnp.exp(masked - top), 0.0)
        total = jnp.sum(block_exp, axis=0, keepdims=True)
        moment = jnp.sum(block_exp * scores, axis=0, keepdims=True)
        part = transposed_left(block_exp.astype(BF16), both[:, width:])
        part_ref[i] = collect_heads(part, masks)
        top_ref[0, i] = jnp.broadcast_to(top, top_ref.shape[2:])
        terms = jnp.concatenate(
            [t.astype(F32) for x in (top, total, moment) for t in split_terms(x)]
            + [jnp.zeros((7, top.shape[1]), F32)],
            0,
        ).astype(BF16)
        wide = transposed_left(terms, place)
        mark = wide[:lats, :LANES]
        for h in range(1, GROUP):
            mark = mark + wide[h * lats : (h + 1) * lats, h * LANES : (h + 1) * LANES]
        mark_ref[i] = mark

    end = message_refs[0].shape[1] - LANES
    for s, message_ref in enumerate(message_refs):
        start = pl.multiple_of(lax.rem(flag_ref[items + 1] + s, frames) * row_total, row_total)
        rows = pl.ds(start, row_total)
        block = jnp.concatenate([part_ref[i, rows, :] for i in range(items)], 0).astype(BF16)
        mark = jnp.concatenate([mark_ref[i, rows, :] for i in range(items)], 0).astype(BF16)
        for g in range(end // width):

            @pl.when(group == g)
            def _():
                message_ref[:, g * width : (g + 1) * width] = block
                if g == 0:
                    message_ref[:, end:] = mark
                else:
                    message_ref[:, end:] = message_ref[:, end:] + mark


def merge_kernel(*refs, chunks, frames, items, head_size, heads):
    message_refs = refs[: chunks * frames]
    base_ref, weight_ref, gain_ref, bias_ref = refs[chunks * frames : chunks * frames + 4]
    merged_ref, mid_ref, ffn_ref, log_ref, entropy_ref = refs[chunks * frames + 4 :]
    own, columns = message_refs[0].shape
    half = columns - LANES
    lane, column = iota((LANES, 3 * LANES), 0), iota((LANES, 3 * LANES), 1)
    gather = jnp.logical_and(
        jnp.logical_and(lane // heads // 3 == column // LANES, lane % heads == column % LANES),
        lane < 9 * heads,
    ).astype(BF16)
    expand = head_expand(half, head_size)
    live = iota((own, LANES), 1) < heads
    spread = jnp.zeros((own, LANES), F32)
    for c in range(chunks):
        sources = message_refs[c * frames : (c + 1) * frames]
        stats = [matmul(x[:, half:], gather) for x in sources]
        tops = [x[:, :LANES] for x in stats]
        peak = functools.reduce(jnp.maximum, tops)
        factors = [jnp.exp(t - peak) for t in tops]
        whole = sum(f * x[:, LANES : 2 * LANES] for f, x in zip(factors, stats))
        moment = sum(f * x[:, 2 * LANES :] for f, x in zip(factors, stats))
        whole = jnp.where(live, whole, 1.0)
        log_total = jnp.where(live, peak + jnp.log(whole), 0.0)
        log_ref[c] = log_total
        spread = spread + jnp.where(live, log_total - moment / whole, 0.0)
        merged = jnp.zeros((own, half), F32)
        for x, factor in zip(sources, factors):
            share = jnp.where(live, factor / whole, 0.0)
            wide = jnp.dot(share, expand, precision=HIGHEST, preferred_element_type=F32)
            merged = merged + x[:, :half].astype(F32) * wide
        merged_ref[:, c * half : (c + 1) * half] = merged
    entropy_ref[...] = jnp.broadcast_to(
        jnp.sum(spread, axis=1, keepdims=True) * (1.0 / HEADS), entropy_ref.shape
    )
    base = jnp.concatenate([base_ref[...]] * items, 0)
    mid = base + matmul(merged_ref[...].astype(BF16), weight_ref[...])
    mid_ref[...] = mid
    ffn_ref[...] = layer_norm(mid, gain_ref[...], bias_ref[...]).astype(BF16)


def gelu_parts(x):
    share = 0.5 * (1.0 + lax.erf(x * (0.5**0.5)))
    slope = share + x * jnp.exp(-0.5 * x * x) * ((2.0 * jnp.pi) ** -0.5)
    return x * share, slope


def feed_kernel(flag_ref, *refs, devices, items):
    row_refs = refs[:devices]
    low_ref, up_ref, down_ref, result_ref = refs[devices : devices + 4]
    grad_refs, (plane_ref, plane_low_ref) = refs[devices + 4 : -2], refs[-2:]
    own, width = row_refs[0].shape
    shard = low_ref.shape[0] // devices
    unit, piece = pack_shape(own, shard, width)
    me = flag_ref[2 * items + 2]
    for d in range(devices):
        plane_ref[d * own : (d + 1) * own, :] = row_refs[d][...]
        source = jnp.bitwise_xor(me, d) * shard
        for a in range(own // unit):
            rows = slice(d * own + a * unit, d * own + (a + 1) * unit)
            for b in range(shard // unit):
                start = pl.multiple_of(source + b * unit, unit)
                plane_low_ref[rows, b * piece : (b + 1) * piece] = low_ref[
                    pl.ds(start, unit), a * piece : (a + 1) * piece
                ]
    upward = matmul(plane_ref[...], up_ref[...])
    hidden, slope = gelu_parts(upward)
    grad_up = (slope * transposed_right(plane_low_ref[...], down_ref[...])).astype(BF16)
    grad = transposed_right(grad_up, up_ref[...]).astype(BF16)
    result = matmul(hidden.astype(BF16), down_ref[...]).astype(BF16)
    for d in range(devices):
        grad_refs[d][...] = grad[d * own : (d + 1) * own, :]
        result_ref[jnp.bitwise_xor(me, d)] = result[d * own : (d + 1) * own, :]


def feed_back_kernel(row_ref, low_ref, up_ref, down_ref, hidden_ref, grad_ref):
    hidden, slope = gelu_parts(matmul(row_ref[...], up_ref[...]))
    hidden_ref[...] = hidden.astype(BF16)
    grad_ref[...] = (slope * transposed_right(low_ref[...], down_ref[...])).astype(BF16)


def outer_kernel(left_ref, right_ref, out_ref):
    out_ref[...] = transposed_left(left_ref[...], right_ref[...]).astype(out_ref.dtype)


def norm_backward(rows, gain, gradient):
    center = rows - jnp.mean(rows, axis=1, keepdims=True)
    rate = lax.rsqrt(jnp.mean(center * center, axis=1, keepdims=True) + EPSILON)
    unit = center * rate
    scaled = gradient * gain
    inner = scaled - jnp.mean(scaled, axis=1, keepdims=True)
    back = rate * (inner - unit * jnp.mean(scaled * unit, axis=1, keepdims=True))
    return (
        back,
        jnp.sum(gradient * unit, axis=0, keepdims=True),
        jnp.sum(gradient, axis=0, keepdims=True),
    )


def turn_kernel(*refs, devices, items, chunks, head_size, heads):
    part_refs = refs[:devices]
    mid_ref, cotangent_ref, gain_ref, merged_ref, log_ref, weight_ref = refs[
        devices : devices + 6
    ]
    message_ref, branch_ref, base_ref, sums_ref = refs[devices + 6 :]
    own, width = mid_ref.shape
    half = width // chunks
    gradient = total_of([x[...] for x in part_refs])
    back, gain_sum, bias_sum = norm_backward(mid_ref[...], gain_ref[...], gradient)
    grad_mid = cotangent_ref[...] + back
    sums_ref[...] = jnp.zeros(sums_ref.shape, F32)
    sums_ref[0:1, :] = gain_sum
    sums_ref[1:2, :] = bias_sum
    row_total = own // items
    base_ref[...] = total_of(
        [grad_mid[i * row_total : (i + 1) * row_total] for i in range(items)]
    )
    branch = grad_mid.astype(BF16)
    branch_ref[:, :width] = branch
    branch_ref[:, width:] = merged_ref[...].astype(BF16)
    grad_att = transposed_right(branch, weight_ref[...]).astype(BF16)
    expand = head_expand(half, head_size)
    lane, column = iota((6 * LANES, LANES), 0), iota((6 * LANES, LANES), 1)
    place = jnp.logical_and(
        lane % LANES < heads, column == (lane // LANES) * heads + lane % LANES
    ).astype(BF16)
    message_ref[:, :width] = grad_att
    for c in range(chunks):
        columns = slice(c * half, (c + 1) * half)
        delta = lax.dot_general(
            merged_ref[:, columns] * grad_att[:, columns].astype(F32),
            expand,
            (((1,), (1,)), ((), ())),
            precision=HIGHEST,
            preferred_element_type=F32,
        )
        terms = jnp.concatenate([t for x in (log_ref[c], delta) for t in split_terms(x)], 1)
        message_ref[:, width + c * LANES : width + (c + 1) * LANES] = matmul(
            terms, place
        ).astype(BF16)


def backward_kernel(
    *refs, frames, items, patches, scale, head_size, heads,
):
    flag_ref, both_ref, query_ref, top_ref = refs[:4]
    grad_refs = refs[4 : 4 + frames]
    mark_refs = refs[4 + frames : 4 + 2 * frames]
    out_ref, sum_ref, held_ref, note_ref = refs[4 + 2 * frames :]
    lats, width = query_ref.shape
    own = grad_refs[0].shape[0]
    row_total = own // items
    base = items * patches
    for s in range(frames):
        source = lax.rem(flag_ref[items + 1] + (frames - s), frames)
        rows = pl.ds(pl.multiple_of(source * row_total, row_total), row_total)
        block = grad_refs[s][...].astype(F32)
        mark = mark_refs[s][...].astype(F32)
        for i in range(items):
            held_ref[i, rows, :] = block[i * row_total : (i + 1) * row_total]
            note_ref[i, rows, :] = mark[i * row_total : (i + 1) * row_total]
    masks = head_masks(lats, width, head_size)
    queries = spread_heads(query_ref[...].astype(F32), masks).astype(BF16)
    lat_both = both_ref[base : base + lats, :]
    row, lane = iota((GROUP * 8, LANES), 0), iota((GROUP * 8, LANES), 1)
    pick = jnp.logical_and(
        jnp.logical_and(
            lane // heads // 3 == row % 8,
            lane % heads == pl.program_id(0) * GROUP + row // 8,
        ),
        lane < 6 * heads,
    ).astype(BF16)
    grad_query = jnp.zeros((queries.shape[0], width), F32)
    lat_grad_key = jnp.zeros((lats, width), F32)
    lat_grad_value = jnp.zeros((lats, width), F32)
    for i in range(items):
        rows = slice(i * patches, (i + 1) * patches)
        stats = transposed_right(pick, note_ref[i].astype(BF16))
        stats = jnp.concatenate([stats[h * 8 : (h + 1) * 8] for h in range(GROUP)], 1)
        log_total = stats[0:1]
        delta = stats[1:2]
        top = top_ref[0, i, 0:1, :]
        rescale = jnp.exp(top - log_total)
        both = jnp.concatenate([both_ref[rows, :], lat_both], 0)
        keys, values = both[:, :width], both[:, width:]
        grads = spread_heads(held_ref[i], masks).astype(BF16)
        live = live_rows(flag_ref, i, items, patches, lats, queries.shape[0])
        masked = jnp.where(live, scale * transposed_right(keys, queries), MASKED)
        probs = jnp.where(live, jnp.exp(masked - log_total), 0.0)
        block_exp = jnp.where(live, jnp.exp(masked - top), 0.0)
        weights = (block_exp.astype(BF16).astype(F32) * rescale).astype(BF16)
        grad_scores = (probs * (transposed_right(values, grads) - delta)).astype(BF16)
        grad_key = scale * matmul(grad_scores, queries)
        grad_value = matmul(weights, grads)
        out_ref[rows, :width] = grad_key[:patches].astype(BF16)
        out_ref[rows, width:] = grad_value[:patches].astype(BF16)
        grad_query = grad_query + transposed_left(grad_scores, keys)
        lat_grad_key = lat_grad_key + grad_key[patches:]
        lat_grad_value = lat_grad_value + grad_value[patches:]
    out_ref[base : base + lats, :width] = lat_grad_key.astype(BF16)
    out_ref[base : base + lats, width:] = lat_grad_value.astype(BF16)
    sum_ref[...] = scale * collect_heads(grad_query, masks)


def media_kernel(flag_ref, *refs, chunks, items, frames):
    grad_refs, lat_refs, weight_refs = [
        refs[k * chunks : (k + 1) * chunks] for k in range(3)
    ]
    media_ref, time_ref, gain_ref, out_ref, sums_ref, product_ref = refs[3 * chunks :]
    item = pl.program_id(0)

    @pl.when(item == 0)
    def _():
        sums_ref[...] = jnp.zeros(sums_ref.shape, F32)
        product_ref[...] = functools.reduce(
            jnp.add, [transposed_right(g[...], w[...]) for g, w in zip(lat_refs, weight_refs)]
        )

    gradient = functools.reduce(
        jnp.add, [transposed_right(g[...], w[...]) for g, w in zip(grad_refs, weight_refs)]
    )
    inputs = media_ref[...].astype(F32) + time_ref[pl.ds(item, 1), :]
    back, gain_sum, bias_sum = norm_backward(inputs, gain_ref[...], gradient)
    out_ref[...] = back.astype(BF16)
    place = iota((frames, 1), 0) == flag_ref[items + 2 + item]
    sums_ref[0:frames, :] += jnp.where(place, jnp.sum(back, axis=0, keepdims=True), 0.0)
    sums_ref[8:9, :] += gain_sum
    sums_ref[9:10, :] += bias_sum


def latent_kernel(flag_ref, *refs, chunks, items):
    query_refs = refs[:chunks]
    (
        product_ref, latent_ref, gain_ref, base_ref, ffn_ref, media_ref, out_ref,
    ) = refs[chunks:]
    lats, width = latent_ref.shape
    half = width // chunks
    gradient = product_ref[...]
    for c in range(chunks):
        out_ref[lats : 2 * lats, c * half : (c + 1) * half] = query_refs[c][...]
    back, gain_sum, bias_sum = norm_backward(latent_ref[...], gain_ref[...], gradient)
    out_ref[:lats, :] = back
    row_total = base_ref.shape[0]
    start = pl.multiple_of(flag_ref[items + 1] * row_total, row_total)
    out_ref[pl.ds(start, row_total), :] += base_ref[...]
    at = 2 * lats
    out_ref[at : at + 8, :] = ffn_ref[...]
    out_ref[at + 2 : at + 3, :] = gain_sum
    out_ref[at + 3 : at + 4, :] = bias_sum
    out_ref[at + 8 : at + 24, :] = media_ref[...]
    out_ref[at + 24 :, :] = jnp.zeros((out_ref.shape[0] - at - 24, width), F32)


def query_norm_kernel(flag_ref, *refs, devices, items):
    column_refs = refs[:devices]
    latent_ref, gain_ref, sum_ref, out_ref, out_gain_ref, out_bias_ref, held_ref = refs[devices:]
    for d in range(devices):
        held_ref[jnp.bitwise_xor(flag_ref[2 * items + 2], d)] = column_refs[d][...]
    gradient = jnp.concatenate([held_ref[k] for k in range(devices)], 1)
    back, gain_sum, bias_sum = norm_backward(latent_ref[...], gain_ref[...], gradient)
    lats = latent_ref.shape[0]
    out_ref[...] = sum_ref[:lats, :] + back
    out_gain_ref[...] = sum_ref[2 * lats + 2 : 2 * lats + 3, :] + gain_sum
    out_bias_ref[...] = sum_ref[2 * lats + 3 : 2 * lats + 4, :] + bias_sum


def rows_kernel(flag_ref, *refs, count, frames, items):
    part_refs, out_refs, held_ref = refs[:count], refs[count:-1], refs[-1]
    rows = held_ref.shape[1]
    column = 0
    for part_ref in part_refs:
        total = total_of([part_ref[k] for k in range(part_ref.shape[0])])
        for f in range(frames):
            held_ref[f, :, column : column + total.shape[1]] = total[f * rows : (f + 1) * rows]
        column += total.shape[1]
    for s, out_ref in enumerate(out_refs):
        block = held_ref[lax.rem(flag_ref[items + 1] + s, frames)]
        out_ref[...] = block.astype(out_ref.dtype)


def place_kernel(flag_ref, *refs, chunks, frames, items, groups):
    chunk_refs = refs[: chunks * frames]
    key_ref, value_ref, out_ref = refs[chunks * frames :]
    width = key_ref.shape[2] // (chunks * groups)
    for s in range(frames):
        source = lax.rem(flag_ref[items + 1] + (frames - s), frames)
        out_ref[source] = chunk_refs[s][:, 2 * groups * width :].astype(F32)
        for c in range(chunks):
            for g in range(groups):
                at = (c * groups + g) * width
                block = chunk_refs[c * frames + s][:, 2 * g * width : 2 * (g + 1) * width]
                block = block.astype(F32)
                key_ref[source, :, at : at + width] = block[:, :width]
                value_ref[source, :, at : at + width] = block[:, width:]


def body(
    media,
    cotangent,
    frame_count,
    frame_start,
    latents,
    time_embed,
    media_gain,
    media_bias,
    latent_gain,
    latent_bias,
    ffn_gain,
    ffn_bias,
    query_weight,
    key_weight,
    value_weight,
    out_weight,
    up_weight,
    down_weight,
):
    items = media.shape[0]
    patches = media.shape[2]
    width = media.shape[3]
    lats = latents.shape[0]
    frame_total = time_embed.shape[0]
    row_total = cotangent.shape[1]
    own = items * row_total
    head_size = width // HEADS
    half = width // CHUNKS
    chunk_heads = HEADS // CHUNKS
    group_width = GROUP * head_size
    groups = chunk_heads // GROUP
    stack = GROUP * lats
    tokens = items * patches
    all_tokens = tokens + lats
    shard = query_weight.shape[0]
    hidden_shard = down_weight.shape[0]
    item_size = lax.axis_size("items")
    frame_size = lax.axis_size("frames")
    plane = item_size * own
    item_index = lax.axis_index("items")
    slot = lax.axis_index("frames")
    row_base = slot * row_total
    params = pltpu.CompilerParams(vmem_limit_bytes=56 * 2**20)
    smem = pl.BlockSpec(memory_space=pltpu.SMEM)
    whole = pl.BlockSpec(memory_space=pltpu.VMEM)
    sizes = dict(items=items, head_size=head_size, heads=chunk_heads)

    def struct(shape, kind):
        return jax.ShapeDtypeStruct(shape, kind)

    def cost(micros):
        return pl.CostEstimate(
            flops=int(micros * 1.15e9), bytes_accessed=int(micros * 3.6e6), transcendentals=0
        )

    def column_blocks(x):
        return jnp.transpose(x.reshape(-1, item_size, shard), (1, 0, 2))

    def scatter_exchange(x, axis):
        return jnp.sum(lax.all_to_all(x, axis, 0, 0).astype(F32), axis=0)

    grad_out = cotangent.reshape(own, width)
    low_columns = own * width // shard
    joined, grad_low = pl.pallas_call(
        functools.partial(join_kernel, width=group_width),
        out_shape=[struct((shard, 2 * width + low_columns), BF16), struct((own, width), BF16)],
        cost_estimate=cost(2.5),
        compiler_params=params,
    )(key_weight, value_weight, grad_out)
    kv_full = lax.all_gather(joined, "items", axis=0, tiled=True)
    low_frames = jnp.stack(spread_on(grad_low, "frames"))

    lat_norm = layer_norm(latents, latent_gain, latent_bias).astype(BF16)
    lat_cols = lax.dynamic_slice_in_dim(lat_norm, item_index * shard, shard, 1)
    query_blocks = column_blocks(matmul(lat_cols, query_weight))
    query_cols = scatter_exchange(query_blocks, "items").astype(BF16)
    query_spread = jnp.broadcast_to(query_cols[None], (item_size, lats, shard))
    queries = jnp.transpose(lax.all_to_all(query_spread, "items", 0, 0), (1, 0, 2)).reshape(
        lats, width
    )

    counts = lax.dynamic_slice_in_dim(frame_count, item_index * items, items)
    starts = lax.dynamic_slice_in_dim(frame_start, item_index * items, items)
    offset = (slot - starts) % frame_total
    flags = jnp.concatenate(
        [
            (offset < counts).astype(jnp.int32),
            (slot == 0).astype(jnp.int32)[None],
            slot.astype(jnp.int32)[None],
            offset.astype(jnp.int32),
            item_index.astype(jnp.int32)[None],
        ]
    )
    picker = (offset[:, None] == jnp.arange(frame_total, dtype=jnp.int32)[None, :]).astype(F32)
    time_rows = jnp.dot(picker, time_embed, precision=HIGHEST, preferred_element_type=F32)
    flat_media = media.reshape(tokens, width)
    steps = tokens // lats
    all_rows = pl.pallas_call(
        functools.partial(norm_kernel, steps=steps, per_item=patches // lats),
        grid=(steps + 1,),
        in_specs=[
            pl.BlockSpec((lats, width), lambda i: (jnp.minimum(i, steps - 1), 0)),
            whole,
            whole,
            whole,
            whole,
        ],
        out_specs=pl.BlockSpec((lats, width), lambda i: (i, 0)),
        out_shape=struct((all_tokens, width), BF16),
        cost_estimate=cost(12),
        compiler_params=params,
    )(
        after(flat_media, query_blocks),
        time_rows,
        media_gain[None],
        media_bias[None],
        lat_norm,
    )
    out_full = lax.all_gather(after(out_weight, all_rows), "items", axis=0, tiled=True)

    core = item_index % 2
    rows_across = after(all_rows, query_cols).T.reshape(item_size // 2, 2, shard, all_tokens)
    send_rows, keep_rows = [
        jnp.concatenate(
            [
                lax.dynamic_slice(
                    rows_across, (k, which, 0, 0), (1, 1, shard, all_tokens)
                ).reshape(shard, all_tokens)
                for k in range(item_size // 2)
            ],
            0,
        )
        for which in (1 - core, core)
    ]
    boths, tops, messages = [], [], []
    for c in range(CHUNKS):

        def block_of(g, c=c):
            return (0, c * groups + g)

        if c:
            rows = after(all_rows, tops[-1])
        else:
            rows = after(all_rows, queries, send_rows, keep_rows)
        both = matmul(rows, kv_full[:, 2 * c * half : 2 * (c + 1) * half]).astype(BF16)
        top, *parts = pl.pallas_call(
            functools.partial(
                forward_kernel, patches=patches, scale=head_size**-0.5, **sizes
            ),
            grid=(groups,),
            in_specs=[
                smem,
                pl.BlockSpec((all_tokens, 2 * group_width), lambda g: (0, g)),
                pl.BlockSpec((lats, group_width), block_of),
            ],
            out_specs=[pl.BlockSpec((1, items, 8, stack), lambda g: (g, 0, 0, 0))]
            + [pl.BlockSpec((own, half + LANES), lambda g: (0, 0))] * frame_size,
            out_shape=[struct((groups, items, 8, stack), F32)]
            + [struct((own, half + LANES), BF16)] * frame_size,
            scratch_shapes=[
                pltpu.VMEM((items, lats, group_width), F32),
                pltpu.VMEM((items, lats, LANES), F32),
            ],
            cost_estimate=cost(7.8),
            compiler_params=params,
        )(flags, both, queries)
        boths.append(both)
        tops.append(top)
        messages += [p if s == 0 else send_on(p, "frames", s) for s, p in enumerate(parts)]
    up_slice = lax.all_to_all(after(up_weight, boths[0]), "items", 1, 0, tiled=True)
    low_all = lax.all_gather(after(low_frames, tops[1]), "items", axis=0).reshape(-1, width)

    base_rows = lax.dynamic_slice_in_dim(latents, row_base, row_total, 0)
    merged, mid_rows, ffn_in, logs, entropy_wide = pl.pallas_call(
        functools.partial(merge_kernel, chunks=CHUNKS, frames=frame_size, **sizes),
        out_shape=[
            struct((own, width), F32),
            struct((own, width), F32),
            struct((own, width), BF16),
            struct((CHUNKS, own, LANES), F32),
            struct((own, LANES), F32),
        ],
        cost_estimate=cost(6.3),
        compiler_params=params,
    )(*messages, base_rows, out_full, ffn_gain[None], ffn_bias[None])
    entropy = entropy_wide[:, 0].reshape(items, row_total)

    ffn_blocks = spread_across(ffn_in, "items")
    ffn_frames = spread_on(after(ffn_in, *ffn_blocks), "frames")
    result_part, *parts = pl.pallas_call(
        functools.partial(feed_kernel, devices=item_size, items=items),
        grid=(1,),
        in_specs=[smem]
        + [whole] * item_size
        + [
            pl.BlockSpec((width, low_columns), lambda i: (0, 2 * width // low_columns)),
            whole,
            whole,
        ],
        out_specs=[whole] * (1 + item_size),
        out_shape=[struct((item_size, own, width), BF16)]
        + [struct((own, width), BF16)] * item_size,
        scratch_shapes=[pltpu.VMEM((plane, width), BF16)] * 2,
        cost_estimate=cost(10),
        compiler_params=params,
    )(flags, *ffn_blocks, kv_full, up_slice, down_weight)
    grad_blocks = collect_across(parts, "items")
    grad_blocks[0] = after(grad_blocks[0], *ffn_frames)

    turn, grad_branch, grad_base, ffn_sums = pl.pallas_call(
        functools.partial(turn_kernel, devices=item_size, chunks=CHUNKS, **sizes),
        out_shape=[
            struct((own, width + CHUNKS * LANES), BF16),
            struct((own, 2 * width), BF16),
            struct((row_total, width), F32),
            struct((8, width), F32),
        ],
        cost_estimate=cost(7.6),
        compiler_params=params,
    )(*grad_blocks, mid_rows, grad_out, ffn_gain[None], merged, logs, out_full)
    turns = spread_on(turn, "frames")
    branch_plane = lax.all_gather(grad_branch, "items", axis=0, tiled=True)
    ffn_all = lax.all_gather(
        after(jnp.stack(ffn_frames), grad_branch), "items", axis=0
    ).reshape(-1, width)
    att_plane = lax.dynamic_slice_in_dim(
        branch_plane, width + item_index * shard, shard, 1
    )
    turns[0] = after(turns[0], low_all)

    chunk_grads, chunk_queries = [], []

    def weight_terms(c):
        send = matmul(send_rows, chunk_grads[c]).astype(BF16)
        received = send_across(send, "items", 1).reshape(-1, shard, 2 * half)
        keep = matmul(after(keep_rows, send), chunk_grads[c]).astype(BF16)
        return send, keep.reshape(-1, shard, 2 * half), received

    def chip_terms(keep, received):
        return (keep.astype(F32) + received.astype(F32)).astype(BF16)

    def exchange_chips(x):
        groups_of = [list(range(k, item_size, 2)) for k in range(2)]
        return lax.all_to_all(x, "items", 0, 0, axis_index_groups=groups_of)

    def frame_rows(ranges):
        rows = shard // frame_size
        columns = sum(x.shape[-1] for x in ranges)
        return pl.pallas_call(
            functools.partial(rows_kernel, count=len(ranges), frames=frame_size, items=items),
            in_specs=[smem] + [whole] * len(ranges),
            out_specs=[whole] * frame_size,
            out_shape=[struct((rows, columns), F32)]
            + [struct((rows, columns), BF16)] * (frame_size - 1),
            scratch_shapes=[pltpu.VMEM((frame_size, rows, columns), F32)],
            cost_estimate=cost(3.5),
            compiler_params=params,
        )(flags, *ranges)

    def send_rows_on(rows):
        return [rows[0]] + [send_on(p, "frames", s) for s, p in enumerate(rows) if s]

    for c in range(CHUNKS):

        def block_of(g, c=c):
            return (0, c * groups + g)

        chunk_grad, chunk_query = pl.pallas_call(
            functools.partial(
                backward_kernel, frames=frame_size, patches=patches, scale=head_size**-0.5, **sizes
            ),
            grid=(groups,),
            in_specs=[
                smem,
                pl.BlockSpec((all_tokens, 2 * group_width), lambda g: (0, g)),
                pl.BlockSpec((lats, group_width), block_of),
                pl.BlockSpec((1, items, 8, stack), lambda g: (g, 0, 0, 0)),
            ]
            + [pl.BlockSpec((own, group_width), block_of)] * frame_size
            + [pl.BlockSpec((own, LANES), lambda g, c=c: (0, width // LANES + c))] * frame_size,
            out_specs=[
                pl.BlockSpec((all_tokens, 2 * group_width), lambda g: (0, g)),
                pl.BlockSpec((lats, group_width), lambda g: (0, g)),
            ],
            out_shape=[
                struct((all_tokens, 2 * half), BF16),
                struct((lats, half), F32),
            ],
            scratch_shapes=[
                pltpu.VMEM((items, lats, group_width), F32),
                pltpu.VMEM((items, lats, LANES), F32),
            ],
            cost_estimate=cost(8),
            compiler_params=params,
        )(flags, after(boths[c], *held) if c else boths[c], queries, tops[c], *turns, *turns)
        chunk_grads.append(chunk_grad)
        chunk_queries.append(chunk_query)
        if c == 0:
            first_send, first_keep, first_received = weight_terms(0)
            held = (first_send,)
    first_terms = chip_terms(after(first_keep, chunk_grads[-1]), first_received)
    first_moved = exchange_chips(first_terms)

    last_block = pl.BlockSpec((lats, 2 * half), lambda i: (tokens // lats, 0))
    media_grad, media_sums, lat_product = pl.pallas_call(
        functools.partial(media_kernel, chunks=CHUNKS, items=items, frames=frame_total),
        grid=(items,),
        in_specs=[smem]
        + [pl.BlockSpec((patches, 2 * half), lambda i: (i, 0))] * CHUNKS
        + [last_block] * CHUNKS
        + [pl.BlockSpec((width, 2 * half), lambda i, c=c: (0, c)) for c in range(CHUNKS)]
        + [pl.BlockSpec((patches, width), lambda i: (i, 0)), whole, whole],
        out_specs=[
            pl.BlockSpec((patches, width), lambda i: (i, 0)),
            pl.BlockSpec((16, width), lambda i: (0, 0)),
            pl.BlockSpec((lats, width), lambda i: (0, 0)),
        ],
        out_shape=[
            struct((tokens, width), BF16),
            struct((16, width), F32),
            struct((lats, width), F32),
        ],
        cost_estimate=cost(21),
        compiler_params=params,
    )(
        flags,
        *chunk_grads[:-1],
        after(chunk_grads[-1], first_terms),
        *chunk_grads,
        *[kv_full] * CHUNKS,
        flat_media,
        time_rows,
        media_gain[None],
    )

    sum_rows = 2 * lats + 24
    sum_rows += -sum_rows % (8 * item_size)
    payload = pl.pallas_call(
        functools.partial(latent_kernel, chunks=CHUNKS, items=items),
        in_specs=[smem] + [whole] * (CHUNKS + 6),
        out_specs=whole,
        out_shape=struct((sum_rows, width), F32),
        cost_estimate=cost(3),
        compiler_params=params,
    )(
        flags,
        *chunk_queries,
        after(lat_product, first_moved),
        latents,
        latent_gain[None],
        grad_base,
        ffn_sums,
        media_sums,
    )
    payload_part = lax.psum_scatter(payload, "items", scatter_dimension=0, tiled=True)

    chunk_grads[-1] = after(chunk_grads[-1], payload)
    last_send, last_keep, last_received = weight_terms(CHUNKS - 1)
    last_terms = chip_terms(after(last_keep, first_moved), last_received)
    last_moved = exchange_chips(last_terms)
    out_part = transposed_left(att_plane, after(branch_plane, last_send)[:, :width])
    first_rows = frame_rows([after(first_moved, last_terms), out_part[None]])
    first_frames = send_rows_on(first_rows)
    all_plane = plane * frame_size
    block_rows = min(512, all_plane)
    row_block = pl.BlockSpec((block_rows, width), lambda i: (i, 0))
    hidden_block = pl.BlockSpec((block_rows, hidden_shard), lambda i: (i, 0))
    hidden, grad_up = pl.pallas_call(
        feed_back_kernel,
        grid=(all_plane // block_rows,),
        in_specs=[row_block, row_block, whole, whole],
        out_specs=[hidden_block, hidden_block],
        out_shape=[struct((all_plane, hidden_shard), BF16)] * 2,
        cost_estimate=cost(15),
        compiler_params=params,
    )(after(ffn_all, *first_rows), low_all, up_slice, down_weight)

    def outer(left, right, tile, kind):
        rows, columns = left.shape
        shape = (columns, right.shape[1])
        return pl.pallas_call(
            outer_kernel,
            grid=(columns // tile,),
            in_specs=[pl.BlockSpec((rows, tile), lambda i: (0, i)), whole],
            out_specs=pl.BlockSpec((tile, shape[1]), lambda i: (i, 0)),
            out_shape=struct(shape, kind),
            cost_estimate=cost(9.5),
            compiler_params=params,
        )(left, right)

    first_total = total_of(first_frames).astype(BF16)
    first_placed = spread_on(first_total, "frames")
    last_rows = frame_rows([after(last_moved, hidden)])
    last_frames = send_rows_on(last_rows)
    up_part = outer(ffn_all, after(grad_up, first_total, *last_rows), width // 4, BF16)
    result_sum = lax.psum_scatter(
        after(result_part, hidden).reshape(-1, width), "items", scatter_dimension=0, tiled=True
    )
    up_moved = lax.all_to_all(up_part, "items", 0, 1, tiled=True)
    up_grad = up_moved.astype(F32)
    last_total = total_of(last_frames).astype(BF16)
    last_placed = spread_on(last_total, "frames")
    down_grad = outer(
        after(hidden, up_part, last_total, *first_placed),
        low_all,
        256 if hidden_shard % 256 == 0 else hidden_shard,
        F32,
    )
    placed = first_placed + last_placed
    payload_part = after(payload_part, last_total)
    payload_others = spread_on(payload_part.astype(BF16), "frames")[1:]
    sums = lax.all_gather(
        total_of([payload_part] + payload_others), "items", axis=0, tiled=True
    )
    query_low = sums[lats : 2 * lats].astype(BF16)
    query_grad = transposed_left(lat_cols, query_low)
    norm_cols = after(transposed_right(query_low, query_weight), up_moved, *last_placed)
    latents_grad, lat_gain, lat_bias = pl.pallas_call(
        functools.partial(query_norm_kernel, devices=item_size, items=items),
        in_specs=[smem] + [whole] * (item_size + 3),
        out_specs=[whole] * 3,
        out_shape=[struct((lats, width), F32), struct((1, width), F32), struct((1, width), F32)],
        scratch_shapes=[pltpu.VMEM((item_size, lats, shard), F32)],
        cost_estimate=cost(3),
        compiler_params=params,
    )(flags, *spread_across(norm_cols, "items"), latents, latent_gain[None], sums)
    at = 2 * lats
    column_sums = lax.dynamic_slice_in_dim(
        sums[at + 8 : at + 24], item_index * shard, shard, 1
    )

    key_grad, value_grad, out_grad = pl.pallas_call(
        functools.partial(
            place_kernel, chunks=CHUNKS, frames=frame_size, items=items, groups=groups
        ),
        in_specs=[smem] + [whole] * len(placed),
        out_specs=[whole] * 3,
        out_shape=[struct((frame_size, shard // frame_size, width), F32)] * 3,
        cost_estimate=cost(3.4),
        compiler_params=params,
    )(flags, *placed)

    result = mid_rows + result_sum.astype(F32)
    return (
        result.reshape(items, row_total, width),
        entropy,
        media_grad.reshape(media.shape),
        latents_grad,
        column_sums[:frame_total],
        column_sums[8],
        column_sums[9],
        lat_gain.reshape(width),
        lat_bias.reshape(width),
        sums[at],
        sums[at + 1],
        query_grad,
        key_grad.reshape(shard, width),
        value_grad.reshape(shard, width),
        out_grad.reshape(shard, width),
        up_grad,
        down_grad,
    )


def solution(mesh):
    return jax.shard_map(
        body,
        mesh=mesh,
        in_specs=(
            P("items", "frames", None, None),
            P("items", "frames", None),
            P(),
            P(),
            P(),
            P(),
            P(),
            P(),
            P(),
            P(),
            P(),
            P(),
            P("items", None),
            P("items", None),
            P("items", None),
            P("items", None),
            P("items", None),
            P("items", None),
        ),
        out_specs=(
            P("items", "frames", None),
            P("items", "frames"),
            P("items", "frames", None, None),
            P(),
            P(None, "items"),
            P("items"),
            P("items"),
            P(),
            P(),
            P(),
            P(),
            P("items", None),
            P("items", None),
            P("items", None),
            P("items", None),
            P("items", None),
            P("items", None),
        ),
        check_vma=False,
    )
```

profile of v0, /device:TPU:0, one launch (start us, length us, event | category | flops | bytes accessed | tf_op | source)
XLA Modules:
  0.0 498.1 jit_solution(9890344444856708280)
XLA Ops:
  7.3 2.7 shard_map.306
  14.1 12.0 %shard_map.305 = bf16[1088,1536]{1,0:T(8,128)(2,1)} custom-call(bf16[1024,1536]{1,0:T(8,128)(2,1)} %bitcast.103, f32[4,1536]{1,0:T(4,128)} %fusion.14.time_ref.refs_7_, f32[1,1536]{1,0:T(1,128)} %broadcast_in_dim.49.gain_ref.refs_8_, f32[1,1536]{1,0:T(1,128)} %broadcast_in_dim.50.bias_ref, bf16[64,1536]{1,0:T(8,128)(2,1)} %copy-done.16), custom_call_target="tpu_custom_call" | custom-call | flops 13799999488 | bytes 43200000 | tf_op jit(solution)/shard_map/pallas_call | solution.py:602
  26.1 5.2 %all-to-all-start = ((f32[8,64,192]{2,1,0:T(8,128)}), f32[8,64,192]{2,1,0:T(8,128)S(1)}, u32[]{:S(2)}, u32[]{:S(2)}) async-start(f32[8,64,192]{2,1,0:T(8,128)} %bitcast.76), calls=%async_computation | async-start | bytes 1048576 | tf_op jit(solution)/shard_map/all_to_all | solution.py:564
  33.0 2.6 collective-permute-start.24
  36.9 5.5 %copy.44 = bf16[1536,1088]{1,0:T(8,128)(2,1)} copy(bf16[1536,1088]{0,1:T(8,128)(2,1)} %bitcast.80) | data formatting | bytes 6684672 | tf_op jit(solution)/shard_map/transpose | solution.py:626
  42.4 3.4 dynamic-slice_bitcast_fusion.7
  48.5 4.1 all-to-all-start.1
  52.7 2.1 pad_maximum_fusion.3
  54.8 7.9 %all-to-all-done.1 = bf16[8,64,192]{2,1,0:T(8,128)(2,1)S(1)} async-done(((bf16[8,64,192]{2,1,0:T(8,128)(2,1)}), bf16[8,64,192]{2,1,0:T(8,128)(2,1)S(1)}, u32[]{:S(2)}, u32[]{:S(2)}) %all-to-all-start.1) | async-done | bytes 196640 | tf_op jit(solution)/shard_map/all_to_all | solution.py:582
  63.7 23.4 %all-gather.9.cloned.1.call-done.refs_8_.refs_4_.refs_5_ = bf16[1536,3584]{1,0:T(8,128)(2,1)} async-done(((bf16[192,3584]{1,0:T(8,128)(2,1)}), bf16[1536,3584]{1,0:T(8,128)(2,1)}) %all-gather.9.cloned.1.call-update) | async-done | bytes 11010064 | tf_op jit(solution)/shard_map/all_gather | solution.py:574
  87.2 9.4 %convolution_convert_fusion.1.both_ref.refs_1_ = bf16[1088,1536]{1,0:T(8,128)(2,1)} fusion(bf16[1088,1536]{1,0:T(8,128)(2,1)} %shard_map.305, bf16[1536,3584]{1,0:T(8,128)(2,1)} %all-gather.9.cloned.1.call-done.refs_8_.refs_4_.refs_5_), kind=kOutput, calls=%fused_computation.1 | convolution fusion | flops 5135499264 | bytes 11403264 | tf_op jit(solution)/shard_map/dot_general | solution.py:29
  96.6 8.0 %shard_map.307 = (f32[2,4,8,256]{3,2,1,0:T(8,128)}, bf16[64,896]{1,0:T(8,128)(2,1)}, bf16[64,896]{1,0:T(8,128)(2,1)}, bf16[64,896]{1,0:T(8,128)(2,1)}, bf16[64,896]{1,0:T(8,128)(2,1)}) custom-call(s32[11]{0:T(128)} %concatenate.9.flag_ref.refs_0_, bf16[1088,1536]{1,0:T(8,128)(2,1)} %convolution_convert_fusion.1.both_ref.refs_1_, ...), custom_call_target="tpu_custom_call" | custom-call | flops 8970000384 | bytes 28080000 | tf_op jit(solution)/shard_map/pallas_call | solution.py:650
  104.6 9.1 %convolution_convert_fusion.both_ref.refs_1_ = bf16[1088,1536]{1,0:T(8,128)(2,1)} fusion(bf16[1088,1536]{1,0:T(8,128)(2,1)S(1)} %copy-done.2, bf16[1536,3584]{1,0:T(8,128)(2,1)} %all-gather.9.cloned.1.call-done.refs_8_.refs_4_.refs_5_), kind=kOutput, calls=%fused_computation | convolution fusion | flops 5135499264 | bytes 11403264 | tf_op jit(solution)/shard_map/dot_general | solution.py:29
  113.6 7.8 %shard_map.308 = (f32[2,4,8,256]{3,2,1,0:T(8,128)}, bf16[64,896]{1,0:T(8,128)(2,1)}, bf16[64,896]{1,0:T(8,128)(2,1)}, bf16[64,896]{1,0:T(8,128)(2,1)}, bf16[64,896]{1,0:T(8,128)(2,1)}) custom-call(s32[11]{0:T(128)} %concatenate.9.flag_ref.refs_0_, bf16[1088,1536]{1,0:T(8,128)(2,1)} %convolution_convert_fusion.both_ref.refs_1_, ...), custom_call_target="tpu_custom_call" | custom-call | flops 8970000384 | bytes 28080000 | tf_op jit(solution)/shard_map/pallas_call | solution.py:650
  123.1 4.2 all-to-all-start.2
  130.0 2.5 collective-permute-start.4
  135.0 2.7 collective-permute-start.2
  138.3 5.8 %collective-permute-done.4.refs_6_ = bf16[64,896]{1,0:T(8,128)(2,1)} collective-permute-done((bf16[64,896]{1,0:T(8,128)(2,1)}, bf16[64,896]{1,0:T(8,128)(2,1)}, u32[]{:S(2)}, u32[]{:S(2)}) %collective-permute-start.4) | collective-permute-done | bytes 114720 | tf_op jit(solution)/shard_map/ppermute | solution.py:46
  144.2 5.6 %collective-permute-done.1.refs_2_ = bf16[64,896]{1,0:T(8,128)(2,1)} collective-permute-done((bf16[64,896]{1,0:T(8,128)(2,1)}, bf16[64,896]{1,0:T(8,128)(2,1)}, u32[]{:S(2)}, u32[]{:S(2)}) %collective-permute-start.1) | collective-permute-done | bytes 114720 | tf_op jit(solution)/shard_map/ppermute | solution.py:46
  149.7 6.3 %shard_map.309 = (f32[64,1536]{1,0:T(8,128)}, f32[64,1536]{1,0:T(8,128)}, bf16[64,1536]{1,0:T(8,128)(2,1)}, f32[2,64,128]{2,1,0:T(8,128)}, f32[64,128]{1,0:T(8,128)}) custom-call(bf16[64,896]{1,0:T(8,128)(2,1)} %get-tuple-element.100.refs_0_, bf16[64,896]{1,0:T(8,128)(2,1)} %collective-permute-done.refs_1_, bf16[64,896]{1,0:T(8,128)(2,1)} %collective-permute-done.1.refs_2_, ...), custom_call_target="tpu_custom_call" | custom-call | flops 7245000192 | bytes 22680000 | tf_op jit(solution)/shard_map/pallas_call | solution.py:678
  159.5 13.8 %collective-permute-done.9.refs_4_ = bf16[64,1536]{1,0:T(8,128)(2,1)S(1)} collective-permute-done((bf16[64,1536]{1,0:T(8,128)(2,1)}, bf16[64,1536]{1,0:T(8,128)(2,1)S(1)}, u32[]{:S(2)}, u32[]{:S(2)}) %collective-permute-start.9) | collective-permute-done | bytes 196640 | tf_op jit(solution)/shard_map/ppermute | solution.py:50
  177.5 1.8 collective-permute-start.14
  181.7 9.8 %shard_map.310 = (bf16[8,64,1536]{2,1,0:T(8,128)(2,1)}, bf16[64,1536]{1,0:T(8,128)(2,1)}, bf16[64,1536]{1,0:T(8,128)(2,1)}, bf16[64,1536]{1,0:T(8,128)(2,1)}, bf...) custom-call(s32[11]{0:T(128)} %concatenate.9.flag_ref.refs_0_, ...), custom_call_target="tpu_custom_call" | custom-call | flops 11500000256 | bytes 36000000 | tf_op jit(solution)/shard_map/pallas_call | solution.py:694
  196.1 3.4 collective-permute-done.17.refs_2_
  199.6 3.3 collective-permute-done.18.refs_3_
  202.9 10.0 %collective-permute-done.20.refs_5_ = bf16[64,1536]{1,0:T(8,128)(2,1)S(1)} collective-permute-done((bf16[64,1536]{1,0:T(8,128)(2,1)}, bf16[64,1536]{1,0:T(8,128)(2,1)S(1)}, u32[]{:S(2)}, u32[]{:S(2)}) %collective-permute-start.20) | collective-permute-done | bytes 196640 | tf_op jit(solution)/shard_map/ppermute | solution.py:50
  213.7 7.6 %shard_map.311 = (bf16[64,1792]{1,0:T(8,128)(2,1)}, bf16[64,3072]{1,0:T(8,128)(2,1)}, f32[16,1536]{1,0:T(8,128)}, f32[8,1536]{1,0:T(8,128)}) custom-call(bf16[64,1536]{1,0:T(8,128)(2,1)} %get-tuple-element.117.refs_0_, bf16[64,1536]{1,0:T(8,128)(2,1)} %copy-done.36, bf16[64,1536]{1,0:T(8,128)(2,1)} %copy-done.38, bf16[64,1536]{1,0:T(8,128)(2,1)} %copy-done.41, ...), custom_call_target="tpu_custom_call" | custom-call | flops 8739999744 | bytes 27360000 | tf_op jit(solution)/shard_map/pallas_call | solution.py:714
  223.7 2.4 collective-permute-start.27
  227.3 5.8 %collective-permute-done.26.refs_5_.refs_9_ = bf16[64,1792]{1,0:T(8,128)(2,1)S(1)} collective-permute-done((bf16[64,1792]{1,0:T(8,128)(2,1)}, bf16[64,1792]{1,0:T(8,128)(2,1)S(1)}, u32[]{:S(2)}, u32[]{:S(2)}) %collective-permute-start.26) | collective-permute-done | bytes 229408 | tf_op jit(solution)/shard_map/ppermute | solution.py:46
  233.0 9.4 %collective-permute-done.27.refs_6_.refs_10_ = bf16[64,1792]{1,0:T(8,128)(2,1)S(1)} collective-permute-done((bf16[64,1792]{1,0:T(8,128)(2,1)}, bf16[64,1792]{1,0:T(8,128)(2,1)S(1)}, u32[]{:S(2)}, u32[]{:S(2)}) %collective-permute-start.27) | collective-permute-done | bytes 229408 | tf_op jit(solution)/shard_map/ppermute | solution.py:46
  243.8 7.9 %shard_map.312 = (bf16[1088,1536]{1,0:T(8,128)(2,1)}, f32[64,768]{1,0:T(8,128)}) custom-call(s32[11]{0:T(128)} %concatenate.9.flag_ref.refs_0_, bf16[1088,1536]{1,0:T(8,128)(2,1)} %convolution_convert_fusion.1.both_ref.refs_1_, bf16[64,1536]{1,0:T(8,128)(2,1)} %reshape.141.query_ref.refs_2_, f32[2,4,8,256]{3,2,1,0:T(8,128)} %get-tuple-element.104.refs_3_, ...), custom_call_target="tpu_custom_call" | custom-call | flops 9200000000 | bytes 28800000 | tf_op jit(solution)/shard_map/pallas_call | solution.py:772
  251.8 6.9 %convolution_convert_fusion.5 = bf16[768,1536]{1,0:T(8,128)(2,1)S(1)} fusion(bf16[1088,1536]{1,0:T(8,128)(2,1)} %get-tuple-element.134.refs_0_.refs_2_, bf16[192,1088]{1,0:T(8,128)(2,1)S(1)} %copy-done.12, bf16[192,1088]{1,0:T(8,128)(2,1)S(1)} %copy-done.13, bf16[192,1088]{1,0:T(8,128)(2,1)S(1)} %copy-done.14, bf16[192,1088]{1,0:T(8,128)(2,1)S(1)} %copy-done.11), kind=kOutput, calls=%fused_computation.11 | convolution fusion | flops 2574778368 | bytes 7372800 | tf_op jit(solution)/shard_map/dot_general | solution.py:29
  259.4 3.4 convolution_convert_fusion.4
  262.8 8.1 %shard_map.313 = (bf16[1088,1536]{1,0:T(8,128)(2,1)}, f32[64,768]{1,0:T(8,128)}) custom-call(s32[11]{0:T(128)} %concatenate.9.flag_ref.refs_0_, bf16[1088,1536]{1,0:T(8,128)(2,1)} %convolution_convert_fusion.both_ref.refs_1_, bf16[64,1536]{1,0:T(8,128)(2,1)} %reshape.141.query_ref.refs_2_, f32[2,4,8,256]{3,2,1,0:T(8,128)} %get-tuple-element.131.refs_3_, ...), custom_call_target="tpu_custom_call" | custom-call | flops 9200000000 | bytes 28800000 | tf_op jit(solution)/shard_map/pallas_call | solution.py:772
  270.9 2.0 fusion.3
  273.0 3.6 all-to-all-start.3
  276.9 21.7 %shard_map.314 = (bf16[1024,1536]{1,0:T(8,128)(2,1)}, f32[16,1536]{1,0:T(8,128)}, f32[64,1536]{1,0:T(8,128)}) custom-call(s32[11]{0:T(128)} %concatenate.9.flag_ref.refs_0_, bf16[1088,1536]{1,0:T(8,128)(2,1)} %get-tuple-element.134.refs_0_.refs_2_, bf16[1088,1536]{1,0:T(8,128)(2,1)} %get-tuple-element.147.refs_1_.refs_3_, ...), custom_call_target="tpu_custom_call" | custom-call | flops 24149999616 | bytes 75600000 | tf_op jit(solution)/shard_map/pallas_call | solution.py:809
  298.6 23.4 %all-to-all-done.3.refs_0_ = bf16[4,192,1536]{2,1,0:T(8,128)(2,1)S(1)} async-done(((bf16[4,192,1536]{2,1,0:T(8,128)(2,1)}), bf16[4,192,1536]{2,1,0:T(8,128)(2,1)S(1)}, u32[]{:S(2)}, u32[]{:S(2)}) %all-to-all-start.3) | async-done | bytes 2359328 | tf_op jit(solution)/shard_map/all_to_all | solution.py:748
  322.0 3.6 shard_map.315
  325.6 7.0 %convolution_convert_fusion.3 = bf16[768,1536]{1,0:T(8,128)(2,1)} fusion(bf16[1088,1536]{1,0:T(8,128)(2,1)} %get-tuple-element.147.refs_1_.refs_3_, bf16[192,1088]{1,0:T(8,128)(2,1)} %get-tuple-element.237, bf16[192,1088]{1,0:T(8,128)(2,1)} %get-tuple-element.238, bf16[192,1088]{1,0:T(8,128)(2,1)} %get-tuple-element.239, bf16[192,1088]{1,0:T(8,128)(2,1)S(1)} %copy-done.11), kind=kOutput, calls=%fused_computation.9 | convolution fusion | flops 2574778368 | bytes 7372800 | tf_op jit(solution)/shard_map/dot_general | solution.py:29
  332.6 7.1 %convolution_convert_fusion.2 = bf16[768,1536]{1,0:T(8,128)(2,1)} fusion(bf16[768,1088]{1,0:T(8,128)(2,1)} %pad_maximum_fusion.1, bf16[1088,1536]{1,0:T(8,128)(2,1)} %get-tuple-element.147.refs_1_.refs_3_), kind=kOutput, calls=%fused_computation.8 | convolution fusion | flops 2568093696 | bytes 7372800 | tf_op jit(solution)/shard_map/dot_general | solution.py:29
  339.7 3.3 convolution_bitcast_fusion.refs_1_
  343.0 2.1 fusion.2
  345.1 3.6 all-to-all-start.4
  348.8 3.8 shard_map.316
  352.6 4.5 collective-permute-start.37
  359.8 14.9 %shard_map.317 = (bf16[2048,768]{1,0:T(8,128)(2,1)}, bf16[2048,768]{1,0:T(8,128)(2,1)}) custom-call(bf16[2048,1536]{1,0:T(8,128)(2,1)} %bitcast.101, bf16[2048,1536]{1,0:T(8,128)(2,1)} %bitcast.99, bf16[1536,768]{1,0:T(8,128)(2,1)} %bitcast.87, bf16[768,1536]{1,0:T(8,128)(2,1)} %down_ref.1), custom_call_target="tpu_custom_call" | custom-call | flops 17250000896 | bytes 54000000 | tf_op jit(solution)/shard_map/pallas_call | solution.py:872
  374.7 5.7 %all-to-all-done.4.refs_0_ = bf16[4,192,1536]{2,1,0:T(8,128)(2,1)S(1)} async-done(((bf16[4,192,1536]{2,1,0:T(8,128)(2,1)}), bf16[4,192,1536]{2,1,0:T(8,128)(2,1)S(1)}, u32[]{:S(2)}, u32[]{:S(2)}) %all-to-all-start.4) | async-done | bytes 2359328 | tf_op jit(solution)/shard_map/all_to_all | solution.py:748
  381.9 3.1 shard_map.318
  384.9 4.5 collective-permute-start.31
  391.8 2.0 add_convert_fusion.refs_0_
  396.4 5.2 %collective-permute-done.32 = bf16[48,1536]{1,0:T(8,128)(2,1)S(1)} collective-permute-done((bf16[48,1536]{1,0:T(8,128)(2,1)}, bf16[48,1536]{1,0:T(8,128)(2,1)S(1)}, u32[]{:S(2)}, u32[]{:S(2)}) %collective-permute-start.32) | collective-permute-done | bytes 147488 | tf_op jit(solution)/shard_map/ppermute | solution.py:46
  403.6 17.2 %collective-permute-start.34 = (bf16[24,1536]{1,0:T(8,128)(2,1)S(1)}, bf16[24,1536]{1,0:T(8,128)(2,1)S(1)}, u32[]{:S(2)}, u32[]{:S(2)}) collective-permute-start(bf16[24,1536]{1,0:T(8,128)(2,1)S(1)} %convert_element_type.122), channel_id=1, source_target_pairs={{0,1},{1,2},{2,3},{3,0},{4,5},{5,6},{6,7},{7,4},{8,9},{9,10},{10,1... | collective-permute-start | bytes 221192 | tf_op jit(solution)/shard_map/ppermute | solution.py:46
  420.8 2.4 collective-permute-start.36
  423.2 9.2 %shard_map.319 = bf16[1536,768]{1,0:T(8,128)(2,1)} custom-call(bf16[2048,1536]{1,0:T(8,128)(2,1)} %bitcast.102, bf16[2048,768]{1,0:T(8,128)(2,1)} %get-tuple-element.168.right_ref), custom_call_target="tpu_custom_call" | custom-call | flops 10924999680 | bytes 34200000 | tf_op jit(solution)/shard_map/pallas_call | solution.py:885
  432.5 3.8 all-to-all-start.5
  436.3 2.0 collective-permute-start.52
  441.3 3.3 collective-permute-start.42
  444.6 6.3 %collective-permute-done.52.refs_3_ = bf16[48,3072]{1,0:T(8,128)(2,1)} collective-permute-done((bf16[48,3072]{1,0:T(8,128)(2,1)}, bf16[48,3072]{1,0:T(8,128)(2,1)}, u32[]{:S(2)}, u32[]{:S(2)}) %collective-permute-start.52) | collective-permute-done | bytes 294944 | tf_op jit(solution)/shard_map/ppermute | solution.py:46
  450.9 9.8 %shard_map.322 = f32[768,1536]{1,0:T(8,128)} custom-call(bf16[2048,768]{1,0:T(8,128)(2,1)} %get-tuple-element.176.left_ref, bf16[2048,1536]{1,0:T(8,128)(2,1)} %bitcast.100), custom_call_target="tpu_custom_call" | custom-call | flops 10924999680 | bytes 34200000 | tf_op jit(solution)/shard_map/pallas_call | solution.py:885
  462.1 3.4 shard_map.321
  467.5 2.7 convert_element_type.130
  476.8 2.5 fusion.7
  485.3 2.9 shard_map.320
  (273 shorter events, 72.4 us)
Async XLA Ops:
  7.2 80.0 %all-gather.9.cloned.1.call-start = ((), (), s32[]{:S(2)}) async-start(), calls=%async_computation.8 | async-start | bytes 12386304 | tf_op jit(solution)/shard_map/all_gather | solution.py:574
  10.0 128.3 %all-gather.11.cloned.1.call-start = ((), (), s32[]{:S(2)}) async-start(), calls=%async_computation.9 | async-start | bytes 5308416 | tf_op jit(solution)/shard_map/all_gather | solution.py:623
  26.1 21.6 %all-to-all-start = ((f32[8,64,192]{2,1,0:T(8,128)}), f32[8,64,192]{2,1,0:T(8,128)S(1)}, u32[]{:S(2)}, u32[]{:S(2)}) async-start(f32[8,64,192]{2,1,0:T(8,128)} %bitcast.76), calls=%async_computation | async-start | bytes 1048576 | tf_op jit(solution)/shard_map/all_to_all | solution.py:564
  31.3 21.3 %collective-permute-start.23 = (bf16[64,1536]{1,0:T(8,128)(2,1)S(1)}, bf16[64,1536]{1,0:T(8,128)(2,1)}, u32[]{:S(2)}, u32[]{:S(2)}) collective-permute-start(bf16[64,1536]{1,0:T(8,128)(2,1)S(1)} %copy-done.18), channel_id=1, source_target_pairs={{0,1},{1,2},{2,3},{3,0},{4,5},{5,6},{6,7},{7,4},{8,9},{9,10},{10,1... | collective-permute-start | bytes 589832 | tf_op jit(solution)/shard_map/ppermute | solution.py:46
  33.0 19.7 %collective-permute-start.24 = (bf16[64,1536]{1,0:T(8,128)(2,1)S(1)}, bf16[64,1536]{1,0:T(8,128)(2,1)}, u32[]{:S(2)}, u32[]{:S(2)}) collective-permute-start(bf16[64,1536]{1,0:T(8,128)(2,1)S(1)} %copy-done.18), channel_id=1, source_target_pairs={{0,2},{1,3},{2,0},{3,1},{4,6},{5,7},{6,4},{7,5},{8,10},{9,11},{10,... | collective-permute-start | bytes 589832 | tf_op jit(solution)/shard_map/ppermute | solution.py:46
  35.6 17.1 %collective-permute-start.25 = (bf16[64,1536]{1,0:T(8,128)(2,1)S(1)}, bf16[64,1536]{1,0:T(8,128)(2,1)}, u32[]{:S(2)}, u32[]{:S(2)}) collective-permute-start(bf16[64,1536]{1,0:T(8,128)(2,1)S(1)} %copy-done.18), channel_id=1, source_target_pairs={{0,3},{1,0},{2,1},{3,2},{4,7},{5,4},{6,5},{7,6},{8,11},{9,8},{10,9... | collective-permute-start | bytes 589832 | tf_op jit(solution)/shard_map/ppermute | solution.py:46
  48.5 14.2 %all-to-all-start.1 = ((bf16[8,64,192]{2,1,0:T(8,128)(2,1)}), bf16[8,64,192]{2,1,0:T(8,128)(2,1)S(1)}, u32[]{:S(2)}, u32[]{:S(2)}) async-start(bf16[8,64,192]{2,1,0:T(8,128)(2,1)} %broadcast_in_dim.51), calls=%async_computation.1 | async-start | bytes 524288 | tf_op jit(solution)/shard_map/all_to_all | solution.py:582
  52.6 174.6 %all-gather.19.cloned.1.call-start = ((), (), s32[]{:S(2)}) async-start(), calls=%async_computation.15 | async-start | bytes 7077888 | tf_op jit(solution)/shard_map/all_gather | solution.py:675
  123.1 57.2 %all-to-all-start.2 = ((bf16[192,8,768]{2,0,1:T(8,128)(2,1)}), bf16[192,8,768]{2,0,1:T(8,128)(2,1)S(1)}, u32[]{:S(2)}, u32[]{:S(2)}) async-start(bf16[192,8,768]{2,0,1:T(8,128)(2,1)} %bitcast.75), calls=%async_computation.2 | async-start | bytes 4718592 | tf_op jit(solution)/shard_map/all_to_all | solution.py:674
  127.3 205.4 %all-gather.13.cloned.1.call-start = ((), (), s32[]{:S(2)}) async-start(), calls=%async_computation.10 | async-start | bytes 3538944 | tf_op jit(solution)/shard_map/all_gather | solution.py:726
  127.3 7.7 %collective-permute-start.3 = (bf16[64,896]{1,0:T(8,128)(2,1)}, bf16[64,896]{1,0:T(8,128)(2,1)}, u32[]{:S(2)}, u32[]{:S(2)}) collective-permute-start(bf16[64,896]{1,0:T(8,128)(2,1)} %get-tuple-element.107), channel_id=1, source_target_pairs={{0,1},{1,2},{2,3},{3,0},{4,5},{5,6},{6,7},{7,4},{8,9},{9,10},{10,1... | collective-permute-start | bytes 344072 | tf_op jit(solution)/shard_map/ppermute | solution.py:46
  130.0 14.2 %collective-permute-start.4 = (bf16[64,896]{1,0:T(8,128)(2,1)}, bf16[64,896]{1,0:T(8,128)(2,1)}, u32[]{:S(2)}, u32[]{:S(2)}) collective-permute-start(bf16[64,896]{1,0:T(8,128)(2,1)} %get-tuple-element.108), channel_id=1, source_target_pairs={{0,2},{1,3},{2,0},{3,1},{4,6},{5,7},{6,4},{7,5},{8,10},{9,11},{10,... | collective-permute-start | bytes 344072 | tf_op jit(solution)/shard_map/ppermute | solution.py:46
  132.4 11.7 %collective-permute-start.5 = (bf16[64,896]{1,0:T(8,128)(2,1)}, bf16[64,896]{1,0:T(8,128)(2,1)}, u32[]{:S(2)}, u32[]{:S(2)}) collective-permute-start(bf16[64,896]{1,0:T(8,128)(2,1)} %get-tuple-element.109), channel_id=1, source_target_pairs={{0,3},{1,0},{2,1},{3,2},{4,7},{5,4},{6,5},{7,6},{8,11},{9,8},{10,9... | collective-permute-start | bytes 344072 | tf_op jit(solution)/shard_map/ppermute | solution.py:46
  133.8 10.3 %collective-permute-start = (bf16[64,896]{1,0:T(8,128)(2,1)}, bf16[64,896]{1,0:T(8,128)(2,1)}, u32[]{:S(2)}, u32[]{:S(2)}) collective-permute-start(bf16[64,896]{1,0:T(8,128)(2,1)} %get-tuple-element.101), channel_id=1, source_target_pairs={{0,1},{1,2},{2,3},{3,0},{4,5},{5,6},{6,7},{7,4},{8,9},{9,10},{10,1... | collective-permute-start | bytes 344072 | tf_op jit(solution)/shard_map/ppermute | solution.py:46
  134.5 15.3 %collective-permute-start.1 = (bf16[64,896]{1,0:T(8,128)(2,1)}, bf16[64,896]{1,0:T(8,128)(2,1)}, u32[]{:S(2)}, u32[]{:S(2)}) collective-permute-start(bf16[64,896]{1,0:T(8,128)(2,1)} %get-tuple-element.102), channel_id=1, source_target_pairs={{0,2},{1,3},{2,0},{3,1},{4,6},{5,7},{6,4},{7,5},{8,10},{9,11},{10,... | collective-permute-start | bytes 344072 | tf_op jit(solution)/shard_map/ppermute | solution.py:46
  135.0 14.7 %collective-permute-start.2 = (bf16[64,896]{1,0:T(8,128)(2,1)S(1)}, bf16[64,896]{1,0:T(8,128)(2,1)}, u32[]{:S(2)}, u32[]{:S(2)}) collective-permute-start(bf16[64,896]{1,0:T(8,128)(2,1)S(1)} %copy-done.52), channel_id=1, source_target_pairs={{0,3},{1,0},{2,1},{3,2},{4,7},{5,4},{6,5},{7,6},{8,11},{9,8},{10,9... | collective-permute-start | bytes 344072 | tf_op jit(solution)/shard_map/ppermute | solution.py:46
  156.0 17.3 %collective-permute-start.9 = (bf16[64,1536]{1,0:T(8,128)(2,1)}, bf16[64,1536]{1,0:T(8,128)(2,1)S(1)}, u32[]{:S(2)}, u32[]{:S(2)}) collective-permute-start(bf16[64,1536]{1,0:T(8,128)(2,1)} %get-tuple-element.115.refs_0_), channel_id=1, source_target_pairs={{0,16},{4,20},{8,24},{12,28},{16,0},{20,4},{24,8},{28,12},{1,17},{... | collective-permute-start | bytes 589832 | tf_op jit(solution)/shard_map/ppermute | solution.py:50
  157.7 15.6 %collective-permute-start.11 = (bf16[64,1536]{1,0:T(8,128)(2,1)}, bf16[64,1536]{1,0:T(8,128)(2,1)S(1)}, u32[]{:S(2)}, u32[]{:S(2)}) collective-permute-start(bf16[64,1536]{1,0:T(8,128)(2,1)} %get-tuple-element.115.refs_0_), channel_id=1, source_target_pairs={{0,24},{4,28},{8,16},{12,20},{16,8},{20,12},{24,0},{28,4},{1,25},{... | collective-permute-start | bytes 589832 | tf_op jit(solution)/shard_map/ppermute | solution.py:50
  159.1 14.6 %collective-permute-start.7 = (bf16[64,1536]{1,0:T(8,128)(2,1)}, bf16[64,1536]{1,0:T(8,128)(2,1)S(1)}, u32[]{:S(2)}, u32[]{:S(2)}) collective-permute-start(bf16[64,1536]{1,0:T(8,128)(2,1)} %get-tuple-element.115.refs_0_), channel_id=1, source_target_pairs={{0,8},{4,12},{8,0},{12,4},{16,24},{20,28},{24,16},{28,20},{1,9},{5... | collective-permute-start | bytes 589832 | tf_op jit(solution)/shard_map/ppermute | solution.py:50
  159.5 14.4 %collective-permute-start.6 = (bf16[64,1536]{1,0:T(8,128)(2,1)}, bf16[64,1536]{1,0:T(8,128)(2,1)S(1)}, u32[]{:S(2)}, u32[]{:S(2)}) collective-permute-start(bf16[64,1536]{1,0:T(8,128)(2,1)} %get-tuple-element.115.refs_0_), channel_id=1, source_target_pairs={{0,4},{4,0},{8,12},{12,8},{16,20},{20,16},{24,28},{28,24},{1,5},{5... | collective-permute-start | bytes 589832 | tf_op jit(solution)/shard_map/ppermute | solution.py:50
  173.3 2.1 collective-permute-start.12
  173.8 2.1 collective-permute-start.8
  175.9 16.8 %collective-permute-start.13 = (bf16[64,1536]{1,0:T(8,128)(2,1)}, bf16[64,1536]{1,0:T(8,128)(2,1)S(1)}, u32[]{:S(2)}, u32[]{:S(2)}) collective-permute-start(bf16[64,1536]{1,0:T(8,128)(2,1)} %get-tuple-element.115.refs_0_), channel_id=1, source_target_pairs={{0,1},{1,2},{2,3},{3,0},{4,5},{5,6},{6,7},{7,4},{8,9},{9,10},{10,1... | collective-permute-start | bytes 589832 | tf_op jit(solution)/shard_map/ppermute | solution.py:46
  177.5 16.0 %collective-permute-start.14 = (bf16[64,1536]{1,0:T(8,128)(2,1)}, bf16[64,1536]{1,0:T(8,128)(2,1)S(1)}, u32[]{:S(2)}, u32[]{:S(2)}) collective-permute-start(bf16[64,1536]{1,0:T(8,128)(2,1)} %get-tuple-element.115.refs_0_), channel_id=1, source_target_pairs={{0,2},{1,3},{2,0},{3,1},{4,6},{5,7},{6,4},{7,5},{8,10},{9,11},{10,... | collective-permute-start | bytes 589832 | tf_op jit(solution)/shard_map/ppermute | solution.py:46
  179.3 15.3 %collective-permute-start.15 = (bf16[64,1536]{1,0:T(8,128)(2,1)}, bf16[64,1536]{1,0:T(8,128)(2,1)S(1)}, u32[]{:S(2)}, u32[]{:S(2)}) collective-permute-start(bf16[64,1536]{1,0:T(8,128)(2,1)} %get-tuple-element.115.refs_0_), channel_id=1, source_target_pairs={{0,3},{1,0},{2,1},{3,2},{4,7},{5,4},{6,5},{7,6},{8,11},{9,8},{10,9... | collective-permute-start | bytes 589832 | tf_op jit(solution)/shard_map/ppermute | solution.py:46
  191.5 3.7 collective-permute-start.16
  191.6 8.0 %collective-permute-start.17 = (bf16[64,1536]{1,0:T(8,128)(2,1)}, bf16[64,1536]{1,0:T(8,128)(2,1)S(1)}, u32[]{:S(2)}, u32[]{:S(2)}) collective-permute-start(bf16[64,1536]{1,0:T(8,128)(2,1)} %get-tuple-element.119), channel_id=1, source_target_pairs={{0,8},{4,12},{8,0},{12,4},{16,24},{20,28},{24,16},{28,20},{1,9},{5... | collective-permute-start | bytes 589832 | tf_op jit(solution)/shard_map/ppermute | solution.py:50
  192.8 10.1 %collective-permute-start.18 = (bf16[64,1536]{1,0:T(8,128)(2,1)}, bf16[64,1536]{1,0:T(8,128)(2,1)S(1)}, u32[]{:S(2)}, u32[]{:S(2)}) collective-permute-start(bf16[64,1536]{1,0:T(8,128)(2,1)} %get-tuple-element.120), channel_id=1, source_target_pairs={{0,12},{4,8},{8,4},{12,0},{16,28},{20,24},{24,20},{28,16},{1,13},{... | collective-permute-start | bytes 589832 | tf_op jit(solution)/shard_map/ppermute | solution.py:50
  193.5 9.4 %collective-permute-start.19 = (bf16[64,1536]{1,0:T(8,128)(2,1)}, bf16[64,1536]{1,0:T(8,128)(2,1)S(1)}, u32[]{:S(2)}, u32[]{:S(2)}) collective-permute-start(bf16[64,1536]{1,0:T(8,128)(2,1)} %get-tuple-element.121), channel_id=1, source_target_pairs={{0,16},{4,20},{8,24},{12,28},{16,0},{20,4},{24,8},{28,12},{1,17},{... | collective-permute-start | bytes 589832 | tf_op jit(solution)/shard_map/ppermute | solution.py:50
  194.6 18.3 %collective-permute-start.20 = (bf16[64,1536]{1,0:T(8,128)(2,1)}, bf16[64,1536]{1,0:T(8,128)(2,1)S(1)}, u32[]{:S(2)}, u32[]{:S(2)}) collective-permute-start(bf16[64,1536]{1,0:T(8,128)(2,1)} %get-tuple-element.122), channel_id=1, source_target_pairs={{0,20},{4,16},{8,28},{12,24},{16,4},{20,0},{24,12},{28,8},{1,21},{... | collective-permute-start | bytes 589832 | tf_op jit(solution)/shard_map/ppermute | solution.py:50
  195.2 17.7 %collective-permute-start.21 = (bf16[64,1536]{1,0:T(8,128)(2,1)}, bf16[64,1536]{1,0:T(8,128)(2,1)S(1)}, u32[]{:S(2)}, u32[]{:S(2)}) collective-permute-start(bf16[64,1536]{1,0:T(8,128)(2,1)} %get-tuple-element.123), channel_id=1, source_target_pairs={{0,24},{4,28},{8,16},{12,20},{16,8},{20,12},{24,0},{28,4},{1,25},{... | collective-permute-start | bytes 589832 | tf_op jit(solution)/shard_map/ppermute | solution.py:50
  199.6 13.3 %collective-permute-start.22 = (bf16[64,1536]{1,0:T(8,128)(2,1)}, bf16[64,1536]{1,0:T(8,128)(2,1)S(1)}, u32[]{:S(2)}, u32[]{:S(2)}) collective-permute-start(bf16[64,1536]{1,0:T(8,128)(2,1)} %get-tuple-element.124), channel_id=1, source_target_pairs={{0,28},{4,24},{8,20},{12,16},{16,12},{20,8},{24,4},{28,0},{1,29},{... | collective-permute-start | bytes 589832 | tf_op jit(solution)/shard_map/ppermute | solution.py:50
  221.4 138.4 %all-gather.17.cloned.1.call-start = ((), (), s32[]{:S(2)}) async-start(), calls=%async_computation.14 | async-start | bytes 7077888 | tf_op jit(solution)/shard_map/all_gather | solution.py:727
  222.4 10.6 %collective-permute-start.26 = (bf16[64,1792]{1,0:T(8,128)(2,1)}, bf16[64,1792]{1,0:T(8,128)(2,1)S(1)}, u32[]{:S(2)}, u32[]{:S(2)}) collective-permute-start(bf16[64,1792]{1,0:T(8,128)(2,1)} %get-tuple-element.133.refs_4_.refs_8_), channel_id=1, source_target_pairs={{0,1},{1,2},{2,3},{3,0},{4,5},{5,6},{6,7},{7,4},{8,9},{9,10},{10,1... | collective-permute-start | bytes 688136 | tf_op jit(solution)/shard_map/ppermute | solution.py:46
  223.7 18.8 %collective-permute-start.27 = (bf16[64,1792]{1,0:T(8,128)(2,1)}, bf16[64,1792]{1,0:T(8,128)(2,1)S(1)}, u32[]{:S(2)}, u32[]{:S(2)}) collective-permute-start(bf16[64,1792]{1,0:T(8,128)(2,1)} %get-tuple-element.133.refs_4_.refs_8_), channel_id=1, source_target_pairs={{0,2},{1,3},{2,0},{3,1},{4,6},{5,7},{6,4},{7,5},{8,10},{9,11},{10,... | collective-permute-start | bytes 688136 | tf_op jit(solution)/shard_map/ppermute | solution.py:46
  226.1 16.4 %collective-permute-start.28 = (bf16[64,1792]{1,0:T(8,128)(2,1)}, bf16[64,1792]{1,0:T(8,128)(2,1)S(1)}, u32[]{:S(2)}, u32[]{:S(2)}) collective-permute-start(bf16[64,1792]{1,0:T(8,128)(2,1)} %get-tuple-element.133.refs_4_.refs_8_), channel_id=1, source_target_pairs={{0,3},{1,0},{2,1},{3,2},{4,7},{5,4},{6,5},{7,6},{8,11},{9,8},{10,9... | collective-permute-start | bytes 688136 | tf_op jit(solution)/shard_map/ppermute | solution.py:46
  258.7 12.3 %collective-permute-start.29 = (bf16[768,1536]{1,0:T(8,128)(2,1)S(1)}, bf16[768,1536]{1,0:T(8,128)(2,1)S(1)}, u32[]{:S(2)}, u32[]{:S(2)}) collective-permute-start(bf16[768,1536]{1,0:T(8,128)(2,1)S(1)} %convolution_convert_fusion.5), channel_id=1, source_target_pairs={{0,4},{4,0},{8,12},{12,8},{16,20},{20,16},{24,28},{28,24},{1,5},{5... | collective-permute-start | bytes 7077896 | tf_op jit(solution)/shard_map/ppermute | solution.py:50
  273.0 49.0 %all-to-all-start.3 = ((bf16[4,192,1536]{2,1,0:T(8,128)(2,1)}), bf16[4,192,1536]{2,1,0:T(8,128)(2,1)S(1)}, u32[]{:S(2)}, u32[]{:S(2)}) async-start(bf16[4,192,1536]{2,1,0:T(8,128)(2,1)} %fusion.3), calls=%async_computation.3 | async-start | bytes 4718592 | tf_op jit(solution)/shard_map/all_to_all | solution.py:748
  276.6 126.0 %reduce-scatter.5.cloned.1.call-start = ((), (), s32[]{:S(2)}) async-start(), calls=%async_computation.12 | async-start | bytes 1327104 | tf_op jit(solution)/shard_map/reduce_scatter | solution.py:859
  332.6 10.4 %collective-permute-start.30 = (bf16[768,1536]{1,0:T(8,128)(2,1)}, bf16[768,1536]{1,0:T(8,128)(2,1)S(1)}, u32[]{:S(2)}, u32[]{:S(2)}) collective-permute-start(bf16[768,1536]{1,0:T(8,128)(2,1)} %convolution_convert_fusion.3), channel_id=1, source_target_pairs={{0,4},{4,0},{8,12},{12,8},{16,20},{20,16},{24,28},{28,24},{1,5},{5... | collective-permute-start | bytes 7077896 | tf_op jit(solution)/shard_map/ppermute | solution.py:50
  345.1 35.4 %all-to-all-start.4 = ((bf16[4,192,1536]{2,1,0:T(8,128)(2,1)}), bf16[4,192,1536]{2,1,0:T(8,128)(2,1)S(1)}, u32[]{:S(2)}, u32[]{:S(2)}) async-start(bf16[4,192,1536]{2,1,0:T(8,128)(2,1)} %fusion.2), calls=%async_computation.6 | async-start | bytes 4718592 | tf_op jit(solution)/shard_map/all_to_all | solution.py:748
  348.7 116.7 %reduce-scatter.3.cloned.1.call-start = ((), (), s32[]{:S(2)}) async-start(), calls=%async_computation.11 | async-start | bytes 1769472 | tf_op jit(solution)/shard_map/reduce_scatter | solution.py:900
  352.6 38.2 %collective-permute-start.37 = (bf16[48,3072]{1,0:T(8,128)(2,1)}, bf16[48,3072]{1,0:T(8,128)(2,1)}, u32[]{:S(2)}, u32[]{:S(2)}) collective-permute-start(bf16[48,3072]{1,0:T(8,128)(2,1)} %get-tuple-element.153), channel_id=1, source_target_pairs={{0,1},{1,2},{2,3},{3,0},{4,5},{5,6},{6,7},{7,4},{8,9},{9,10},{10,1... | collective-permute-start | bytes 884744 | tf_op jit(solution)/shard_map/ppermute | solution.py:46
  357.2 34.6 %collective-permute-start.38 = (bf16[48,3072]{1,0:T(8,128)(2,1)}, bf16[48,3072]{1,0:T(8,128)(2,1)}, u32[]{:S(2)}, u32[]{:S(2)}) collective-permute-start(bf16[48,3072]{1,0:T(8,128)(2,1)} %get-tuple-element.154), channel_id=1, source_target_pairs={{0,2},{1,3},{2,0},{3,1},{4,6},{5,7},{6,4},{7,5},{8,10},{9,11},{10,... | collective-permute-start | bytes 884744 | tf_op jit(solution)/shard_map/ppermute | solution.py:46
  358.5 33.3 %collective-permute-start.39 = (bf16[48,3072]{1,0:T(8,128)(2,1)}, bf16[48,3072]{1,0:T(8,128)(2,1)}, u32[]{:S(2)}, u32[]{:S(2)}) collective-permute-start(bf16[48,3072]{1,0:T(8,128)(2,1)} %get-tuple-element.155), channel_id=1, source_target_pairs={{0,3},{1,0},{2,1},{3,2},{4,7},{5,4},{6,5},{7,6},{8,11},{9,8},{10,9... | collective-permute-start | bytes 884744 | tf_op jit(solution)/shard_map/ppermute | solution.py:46
  384.9 11.5 %collective-permute-start.31 = (bf16[48,1536]{1,0:T(8,128)(2,1)}, bf16[48,1536]{1,0:T(8,128)(2,1)S(1)}, u32[]{:S(2)}, u32[]{:S(2)}) collective-permute-start(bf16[48,1536]{1,0:T(8,128)(2,1)} %get-tuple-element.163), channel_id=1, source_target_pairs={{0,1},{1,2},{2,3},{3,0},{4,5},{5,6},{6,7},{7,4},{8,9},{9,10},{10,1... | collective-permute-start | bytes 442376 | tf_op jit(solution)/shard_map/ppermute | solution.py:46
  389.4 12.1 %collective-permute-start.32 = (bf16[48,1536]{1,0:T(8,128)(2,1)}, bf16[48,1536]{1,0:T(8,128)(2,1)S(1)}, u32[]{:S(2)}, u32[]{:S(2)}) collective-permute-start(bf16[48,1536]{1,0:T(8,128)(2,1)} %get-tuple-element.164), channel_id=1, source_target_pairs={{0,2},{1,3},{2,0},{3,1},{4,6},{5,7},{6,4},{7,5},{8,10},{9,11},{10,... | collective-permute-start | bytes 442376 | tf_op jit(solution)/shard_map/ppermute | solution.py:46
  390.8 10.7 %collective-permute-start.33 = (bf16[48,1536]{1,0:T(8,128)(2,1)}, bf16[48,1536]{1,0:T(8,128)(2,1)S(1)}, u32[]{:S(2)}, u32[]{:S(2)}) collective-permute-start(bf16[48,1536]{1,0:T(8,128)(2,1)} %get-tuple-element.165), channel_id=1, source_target_pairs={{0,3},{1,0},{2,1},{3,2},{4,7},{5,4},{6,5},{7,6},{8,11},{9,8},{10,9... | collective-permute-start | bytes 442376 | tf_op jit(solution)/shard_map/ppermute | solution.py:46
  393.8 47.5 %collective-permute-start.50 = (bf16[48,3072]{1,0:T(8,128)(2,1)}, bf16[48,3072]{1,0:T(8,128)(2,1)}, u32[]{:S(2)}, u32[]{:S(2)}) collective-permute-start(bf16[48,3072]{1,0:T(8,128)(2,1)} %add_convert_fusion.refs_0_), channel_id=1, source_target_pairs={{0,1},{1,2},{2,3},{3,0},{4,5},{5,6},{6,7},{7,4},{8,9},{9,10},{10,1... | collective-permute-start | bytes 884744 | tf_op jit(solution)/shard_map/ppermute | solution.py:46
  394.9 49.7 %collective-permute-start.51 = (bf16[48,3072]{1,0:T(8,128)(2,1)}, bf16[48,3072]{1,0:T(8,128)(2,1)}, u32[]{:S(2)}, u32[]{:S(2)}) collective-permute-start(bf16[48,3072]{1,0:T(8,128)(2,1)} %add_convert_fusion.refs_0_), channel_id=1, source_target_pairs={{0,2},{1,3},{2,0},{3,1},{4,6},{5,7},{6,4},{7,5},{8,10},{9,11},{10,... | collective-permute-start | bytes 884744 | tf_op jit(solution)/shard_map/ppermute | solution.py:46
  403.6 32.7 %collective-permute-start.34 = (bf16[24,1536]{1,0:T(8,128)(2,1)S(1)}, bf16[24,1536]{1,0:T(8,128)(2,1)S(1)}, u32[]{:S(2)}, u32[]{:S(2)}) collective-permute-start(bf16[24,1536]{1,0:T(8,128)(2,1)S(1)} %convert_element_type.122), channel_id=1, source_target_pairs={{0,1},{1,2},{2,3},{3,0},{4,5},{5,6},{6,7},{7,4},{8,9},{9,10},{10,1... | collective-permute-start | bytes 221192 | tf_op jit(solution)/shard_map/ppermute | solution.py:46
  420.8 17.5 %collective-permute-start.35 = (bf16[24,1536]{1,0:T(8,128)(2,1)S(1)}, bf16[24,1536]{1,0:T(8,128)(2,1)S(1)}, u32[]{:S(2)}, u32[]{:S(2)}) collective-permute-start(bf16[24,1536]{1,0:T(8,128)(2,1)S(1)} %convert_element_type.122), channel_id=1, source_target_pairs={{0,2},{1,3},{2,0},{3,1},{4,6},{5,7},{6,4},{7,5},{8,10},{9,11},{10,... | collective-permute-start | bytes 221192 | tf_op jit(solution)/shard_map/ppermute | solution.py:46
  420.8 17.5 %collective-permute-start.36 = (bf16[24,1536]{1,0:T(8,128)(2,1)S(1)}, bf16[24,1536]{1,0:T(8,128)(2,1)}, u32[]{:S(2)}, u32[]{:S(2)}) collective-permute-start(bf16[24,1536]{1,0:T(8,128)(2,1)S(1)} %convert_element_type.122), channel_id=1, source_target_pairs={{0,3},{1,0},{2,1},{3,2},{4,7},{5,4},{6,5},{7,6},{8,11},{9,8},{10,9... | collective-permute-start | bytes 221192 | tf_op jit(solution)/shard_map/ppermute | solution.py:46
  432.5 34.7 %all-to-all-start.5 = ((bf16[8,192,768]{2,1,0:T(8,128)(2,1)}), bf16[8,192,768]{2,1,0:T(8,128)(2,1)S(1)}, u32[]{:S(2)}, u32[]{:S(2)}) async-start(bf16[8,192,768]{2,1,0:T(8,128)(2,1)} %bitcast.88), calls=%async_computation.7 | async-start | bytes 4718592 | tf_op jit(solution)/shard_map/all_to_all | solution.py:903
  436.2 35.7 %all-gather.15.cloned.1.call-start = ((), (), s32[]{:S(2)}) async-start(), calls=%async_computation.13 | async-start | bytes 1327104 | tf_op jit(solution)/shard_map/all_gather | solution.py:916
  436.3 14.6 %collective-permute-start.52 = (bf16[48,3072]{1,0:T(8,128)(2,1)}, bf16[48,3072]{1,0:T(8,128)(2,1)}, u32[]{:S(2)}, u32[]{:S(2)}) collective-permute-start(bf16[48,3072]{1,0:T(8,128)(2,1)} %add_convert_fusion.refs_0_), channel_id=1, source_target_pairs={{0,3},{1,0},{2,1},{3,2},{4,7},{5,4},{6,5},{7,6},{8,11},{9,8},{10,9... | collective-permute-start | bytes 884744 | tf_op jit(solution)/shard_map/ppermute | solution.py:46
  440.7 20.0 %collective-permute-start.40 = (bf16[48,1536]{1,0:T(8,128)(2,1)S(1)}, bf16[48,1536]{1,0:T(8,128)(2,1)S(1)}, u32[]{:S(2)}, u32[]{:S(2)}) collective-permute-start(bf16[48,1536]{1,0:T(8,128)(2,1)S(1)} %add_convert_fusion.2.refs_4_), channel_id=1, source_target_pairs={{0,1},{1,2},{2,3},{3,0},{4,5},{5,6},{6,7},{7,4},{8,9},{9,10},{10,1... | collective-permute-start | bytes 442376 | tf_op jit(solution)/shard_map/ppermute | solution.py:46
  440.8 19.9 %collective-permute-start.41 = (bf16[48,1536]{1,0:T(8,128)(2,1)S(1)}, bf16[48,1536]{1,0:T(8,128)(2,1)S(1)}, u32[]{:S(2)}, u32[]{:S(2)}) collective-permute-start(bf16[48,1536]{1,0:T(8,128)(2,1)S(1)} %add_convert_fusion.2.refs_4_), channel_id=1, source_target_pairs={{0,2},{1,3},{2,0},{3,1},{4,6},{5,7},{6,4},{7,5},{8,10},{9,11},{10,... | collective-permute-start | bytes 442376 | tf_op jit(solution)/shard_map/ppermute | solution.py:46
  441.3 19.4 %collective-permute-start.42 = (bf16[48,1536]{1,0:T(8,128)(2,1)S(1)}, bf16[48,1536]{1,0:T(8,128)(2,1)S(1)}, u32[]{:S(2)}, u32[]{:S(2)}) collective-permute-start(bf16[48,1536]{1,0:T(8,128)(2,1)S(1)} %add_convert_fusion.2.refs_4_), channel_id=1, source_target_pairs={{0,3},{1,0},{2,1},{3,2},{4,7},{5,4},{6,5},{7,6},{8,11},{9,8},{10,9... | collective-permute-start | bytes 442376 | tf_op jit(solution)/shard_map/ppermute | solution.py:46
  473.2 9.1 %collective-permute-start.44 = (f32[64,192]{1,0:T(8,128)S(1)}, f32[64,192]{1,0:T(8,128)S(1)}, u32[]{:S(2)}, u32[]{:S(2)}) collective-permute-start(f32[64,192]{1,0:T(8,128)S(1)} %fusion.6.refs_0_), channel_id=1, source_target_pairs={{0,8},{4,12},{8,0},{12,4},{16,24},{20,28},{24,16},{28,20},{1,9},{5... | collective-permute-start | bytes 147464 | tf_op jit(solution)/shard_map/ppermute | solution.py:50
  474.6 8.2 %collective-permute-start.46 = (f32[64,192]{1,0:T(8,128)S(1)}, f32[64,192]{1,0:T(8,128)S(1)}, u32[]{:S(2)}, u32[]{:S(2)}) collective-permute-start(f32[64,192]{1,0:T(8,128)S(1)} %fusion.6.refs_0_), channel_id=1, source_target_pairs={{0,16},{4,20},{8,24},{12,28},{16,0},{20,4},{24,8},{28,12},{1,17},{... | collective-permute-start | bytes 147464 | tf_op jit(solution)/shard_map/ppermute | solution.py:50
  475.2 7.7 %collective-permute-start.48 = (f32[64,192]{1,0:T(8,128)S(1)}, f32[64,192]{1,0:T(8,128)S(1)}, u32[]{:S(2)}, u32[]{:S(2)}) collective-permute-start(f32[64,192]{1,0:T(8,128)S(1)} %fusion.6.refs_0_), channel_id=1, source_target_pairs={{0,24},{4,28},{8,16},{12,20},{16,8},{20,12},{24,0},{28,4},{1,25},{... | collective-permute-start | bytes 147464 | tf_op jit(solution)/shard_map/ppermute | solution.py:50
  476.8 7.2 %collective-permute-start.43 = (f32[64,192]{1,0:T(8,128)S(1)}, f32[64,192]{1,0:T(8,128)S(1)}, u32[]{:S(2)}, u32[]{:S(2)}) collective-permute-start(f32[64,192]{1,0:T(8,128)S(1)} %fusion.6.refs_0_), channel_id=1, source_target_pairs={{0,4},{4,0},{8,12},{12,8},{16,20},{20,16},{24,28},{28,24},{1,5},{5... | collective-permute-start | bytes 147464 | tf_op jit(solution)/shard_map/ppermute | solution.py:50
  482.3 1.7 collective-permute-start.45
  (65 other events, 437.6 us)
Sparse Core Ops, SparseCore 0:
  10.5 76.6 all-gather.8
  89.0 38.9 all-gather.10
  130.5 64.5 all-gather.18
  221.5 32.3 all-gather.12
  256.2 67.5 all-gather.16
  339.8 53.6 reduce-scatter.4
  397.2 38.4 reduce-scatter.2
  440.0 31.8 all-gather.14
where the time goes:
time: 508 us; the launch traced here: 498 us
  Pallas kernels  143 us (28%)
  waiting for transfers between devices  133 us (26%)
  starting transfers between devices  104 us (20%)
  matrix products  51 us (10%)
  local copies, waits for them, and re-layouts  29.7 us (6%)
  other arithmetic  21.7 us (4%)
  between operations  15.2 us (3%)
    ppermute x30, starting transfers between devices, send_on(): return lax.ppermute(x, axis, [(i, (i + step) % size) for i in range(size)])  65.8 us
    dot_general x7, matrix products, matmul(): return jnp.dot(left_side, right_side, preferred_element_type=F32)  43.1 us
    ppermute x30, waiting for transfers between devices, send_on(): return lax.ppermute(x, axis, [(i, (i + step) % size) for i in range(size)])  38.3 us
    ppermute x23, waiting for transfers between devices, send_across(): lax.ppermute(x, axis, [(i, i ^ distance) for i in range(lax.axis_size(axi...  32.8 us
    all_to_all x2, waiting for transfers between devices, exchange_chips(): return lax.all_to_all(x, 'items', 0, 0, axis_index_groups=groups_of)  29.1 us
    all_gather x1, waiting for transfers between devices, body(): kv_full = lax.all_gather(joined, 'items', axis=0, tiled=True)  23.4 us
    pallas_call x1, Pallas kernels, body(): pl.pallas_call(functools.partial(media_kernel, chunks=CHUNKS, items=items...  21.7 us
    pallas_call x2, Pallas kernels, outer(): pl.pallas_call(outer_kernel, grid=(columns // tile,), in_specs=[pl.BlockS...  19 us
  transfers between devices with their start and end apart: 67, of which 22 were waited for; matrix products, arithmetic and copies ran while one was open for 18% of the time, Pallas kernels for 28%

commit v1 on v0

--- a/solution.py
+++ b/solution.py
@@ -911,7 +911,7 @@
         F32,
     )
     placed = first_placed + last_placed
-    payload_part = after(payload_part, last_total)
+    payload_part = after(payload_part, last_total, up_part)
     payload_others = spread_on(payload_part.astype(BF16), "frames")[1:]
     sums = lax.all_gather(
         total_of([payload_part] + payload_others), "items", axis=0, tiled=True

time: 508 us -> 510 us (level)
  waiting for transfers between devices: 133 us -> 146 us
  starting transfers between devices: 104 us -> 93.4 us
    all_gather x1, waiting for transfers between devices: 1.72 us -> 12.4 us  [body(): lax.all_gather(total_of([payload_part] + payload_others), 'items', axis=0...]
    ppermute x30, starting transfers between devices: 65.8 us -> 55.3 us  [send_on(): return lax.ppermute(x, axis, [(i, (i + step) % size) for i in range(size)])]
    ppermute x30, waiting for transfers between devices: 38.3 us -> 46 us  [send_on(): return lax.ppermute(x, axis, [(i, (i + step) % size) for i in range(size)])]
    all_to_all x2, waiting for transfers between devices: 29.1 us -> 23.3 us  [exchange_chips(): return lax.all_to_all(x, 'items', 0, 0, axis_index_groups=groups_of)]
  transfers between devices with their start and end apart: 67 -> 67, of which waited for: 22 -> 22; matrix products, arithmetic and copies ran while one was open for 18% -> 18% of each run, Pallas kernels for 28% -> 27%
where the time goes in v1:
time: 510 us; the launch traced here: 501 us
  waiting for transfers between devices  146 us (29%)
  Pallas kernels  143 us (28%)
  starting transfers between devices  93.4 us (18%)
  matrix products  51 us (10%)
  local copies, waits for them, and re-layouts  30.5 us (6%)
  other arithmetic  21.5 us (4%)
  between operations  15.2 us (3%)
    ppermute x30, starting transfers between devices, send_on(): return lax.ppermute(x, axis, [(i, (i + step) % size) for i in range(size)])  55.3 us
    ppermute x30, waiting for transfers between devices, send_on(): return lax.ppermute(x, axis, [(i, (i + step) % size) for i in range(size)])  46 us
    dot_general x7, matrix products, matmul(): return jnp.dot(left_side, right_side, preferred_element_type=F32)  43.1 us
    ppermute x23, waiting for transfers between devices, send_across(): lax.ppermute(x, axis, [(i, i ^ distance) for i in range(lax.axis_size(axi...  32.8 us
    all_gather x1, waiting for transfers between devices, body(): kv_full = lax.all_gather(joined, 'items', axis=0, tiled=True)  23.4 us
    all_to_all x2, waiting for transfers between devices, exchange_chips(): return lax.all_to_all(x, 'items', 0, 0, axis_index_groups=groups_of)  23.3 us
    pallas_call x1, Pallas kernels, body(): pl.pallas_call(functools.partial(media_kernel, chunks=CHUNKS, items=items...  21.8 us
    pallas_call x2, Pallas kernels, outer(): pl.pallas_call(outer_kernel, grid=(columns // tile,), in_specs=[pl.BlockS...  19 us
  transfers between devices with their start and end apart: 67, of which 22 were waited for; matrix products, arithmetic and copies ran while one was open for 18% of the time, Pallas kernels for 27%

profile of v1, /device:TPU:0, one launch (start us, length us, event | category | flops | bytes accessed | tf_op | source)
XLA Modules:
  0.0 500.6 jit_solution(893112134657200183)
XLA Ops:
  7.3 2.7 shard_map.306
  14.1 12.0 %shard_map.305 = bf16[1088,1536]{1,0:T(8,128)(2,1)} custom-call(bf16[1024,1536]{1,0:T(8,128)(2,1)} %bitcast.103, f32[4,1536]{1,0:T(4,128)} %fusion.14.time_ref.refs_7_, f32[1,1536]{1,0:T(1,128)} %broadcast_in_dim.49.gain_ref.refs_8_, f32[1,1536]{1,0:T(1,128)} %broadcast_in_dim.50.bias_ref, bf16[64,1536]{1,0:T(8,128)(2,1)} %copy-done.16), custom_call_target="tpu_custom_call" | custom-call | flops 13799999488 | bytes 43200000 | tf_op jit(solution)/shard_map/pallas_call | solution.py:602
  26.1 5.2 %all-to-all-start = ((f32[8,64,192]{2,1,0:T(8,128)}), f32[8,64,192]{2,1,0:T(8,128)S(1)}, u32[]{:S(2)}, u32[]{:S(2)}) async-start(f32[8,64,192]{2,1,0:T(8,128)} %bitcast.76), calls=%async_computation | async-start | bytes 1048576 | tf_op jit(solution)/shard_map/all_to_all | solution.py:564
  32.9 2.6 collective-permute-start.24
  36.9 5.5 %copy.44 = bf16[1536,1088]{1,0:T(8,128)(2,1)} copy(bf16[1536,1088]{0,1:T(8,128)(2,1)} %bitcast.80) | data formatting | bytes 6684672 | tf_op jit(solution)/shard_map/transpose | solution.py:626
  42.4 3.4 dynamic-slice_bitcast_fusion.7
  48.5 4.1 all-to-all-start.1
  52.7 2.1 pad_maximum_fusion.3
  54.8 7.9 %all-to-all-done.1 = bf16[8,64,192]{2,1,0:T(8,128)(2,1)S(1)} async-done(((bf16[8,64,192]{2,1,0:T(8,128)(2,1)}), bf16[8,64,192]{2,1,0:T(8,128)(2,1)S(1)}, u32[]{:S(2)}, u32[]{:S(2)}) %all-to-all-start.1) | async-done | bytes 196640 | tf_op jit(solution)/shard_map/all_to_all | solution.py:582
  63.7 23.4 %all-gather.9.cloned.1.call-done.refs_8_.refs_4_.refs_5_ = bf16[1536,3584]{1,0:T(8,128)(2,1)} async-done(((bf16[192,3584]{1,0:T(8,128)(2,1)}), bf16[1536,3584]{1,0:T(8,128)(2,1)}) %all-gather.9.cloned.1.call-update) | async-done | bytes 11010064 | tf_op jit(solution)/shard_map/all_gather | solution.py:574
  87.2 9.4 %convolution_convert_fusion.1.both_ref.refs_1_ = bf16[1088,1536]{1,0:T(8,128)(2,1)} fusion(bf16[1088,1536]{1,0:T(8,128)(2,1)} %shard_map.305, bf16[1536,3584]{1,0:T(8,128)(2,1)} %all-gather.9.cloned.1.call-done.refs_8_.refs_4_.refs_5_), kind=kOutput, calls=%fused_computation.1 | convolution fusion | flops 5135499264 | bytes 11403264 | tf_op jit(solution)/shard_map/dot_general | solution.py:29
  96.6 8.0 %shard_map.307 = (f32[2,4,8,256]{3,2,1,0:T(8,128)}, bf16[64,896]{1,0:T(8,128)(2,1)}, bf16[64,896]{1,0:T(8,128)(2,1)}, bf16[64,896]{1,0:T(8,128)(2,1)}, bf16[64,896]{1,0:T(8,128)(2,1)}) custom-call(s32[11]{0:T(128)} %concatenate.9.flag_ref.refs_0_, bf16[1088,1536]{1,0:T(8,128)(2,1)} %convolution_convert_fusion.1.both_ref.refs_1_, ...), custom_call_target="tpu_custom_call" | custom-call | flops 8970000384 | bytes 28080000 | tf_op jit(solution)/shard_map/pallas_call | solution.py:650
  104.6 9.1 %convolution_convert_fusion.both_ref.refs_1_ = bf16[1088,1536]{1,0:T(8,128)(2,1)} fusion(bf16[1088,1536]{1,0:T(8,128)(2,1)S(1)} %copy-done.2, bf16[1536,3584]{1,0:T(8,128)(2,1)} %all-gather.9.cloned.1.call-done.refs_8_.refs_4_.refs_5_), kind=kOutput, calls=%fused_computation | convolution fusion | flops 5135499264 | bytes 11403264 | tf_op jit(solution)/shard_map/dot_general | solution.py:29
  113.6 7.9 %shard_map.308 = (f32[2,4,8,256]{3,2,1,0:T(8,128)}, bf16[64,896]{1,0:T(8,128)(2,1)}, bf16[64,896]{1,0:T(8,128)(2,1)}, bf16[64,896]{1,0:T(8,128)(2,1)}, bf16[64,896]{1,0:T(8,128)(2,1)}) custom-call(s32[11]{0:T(128)} %concatenate.9.flag_ref.refs_0_, bf16[1088,1536]{1,0:T(8,128)(2,1)} %convolution_convert_fusion.both_ref.refs_1_, ...), custom_call_target="tpu_custom_call" | custom-call | flops 8970000384 | bytes 28080000 | tf_op jit(solution)/shard_map/pallas_call | solution.py:650
  123.1 4.2 all-to-all-start.2
  130.0 2.5 collective-permute-start.4
  135.1 2.7 collective-permute-start.2
  138.4 5.8 %collective-permute-done.4.refs_6_ = bf16[64,896]{1,0:T(8,128)(2,1)} collective-permute-done((bf16[64,896]{1,0:T(8,128)(2,1)}, bf16[64,896]{1,0:T(8,128)(2,1)}, u32[]{:S(2)}, u32[]{:S(2)}) %collective-permute-start.4) | collective-permute-done | bytes 114720 | tf_op jit(solution)/shard_map/ppermute | solution.py:46
  144.2 5.6 %collective-permute-done.1.refs_2_ = bf16[64,896]{1,0:T(8,128)(2,1)} collective-permute-done((bf16[64,896]{1,0:T(8,128)(2,1)}, bf16[64,896]{1,0:T(8,128)(2,1)}, u32[]{:S(2)}, u32[]{:S(2)}) %collective-permute-start.1) | collective-permute-done | bytes 114720 | tf_op jit(solution)/shard_map/ppermute | solution.py:46
  149.8 6.3 %shard_map.309 = (f32[64,1536]{1,0:T(8,128)}, f32[64,1536]{1,0:T(8,128)}, bf16[64,1536]{1,0:T(8,128)(2,1)}, f32[2,64,128]{2,1,0:T(8,128)}, f32[64,128]{1,0:T(8,128)}) custom-call(bf16[64,896]{1,0:T(8,128)(2,1)} %get-tuple-element.100.refs_0_, bf16[64,896]{1,0:T(8,128)(2,1)} %collective-permute-done.refs_1_, bf16[64,896]{1,0:T(8,128)(2,1)} %collective-permute-done.1.refs_2_, ...), custom_call_target="tpu_custom_call" | custom-call | flops 7245000192 | bytes 22680000 | tf_op jit(solution)/shard_map/pallas_call | solution.py:678
  159.5 13.8 %collective-permute-done.9.refs_4_ = bf16[64,1536]{1,0:T(8,128)(2,1)S(1)} collective-permute-done((bf16[64,1536]{1,0:T(8,128)(2,1)}, bf16[64,1536]{1,0:T(8,128)(2,1)S(1)}, u32[]{:S(2)}, u32[]{:S(2)}) %collective-permute-start.9) | collective-permute-done | bytes 196640 | tf_op jit(solution)/shard_map/ppermute | solution.py:50
  181.7 9.8 %shard_map.310 = (bf16[8,64,1536]{2,1,0:T(8,128)(2,1)}, bf16[64,1536]{1,0:T(8,128)(2,1)}, bf16[64,1536]{1,0:T(8,128)(2,1)}, bf16[64,1536]{1,0:T(8,128)(2,1)}, bf...) custom-call(s32[11]{0:T(128)} %concatenate.9.flag_ref.refs_0_, ...), custom_call_target="tpu_custom_call" | custom-call | flops 11500000256 | bytes 36000000 | tf_op jit(solution)/shard_map/pallas_call | solution.py:694
  196.1 3.5 collective-permute-done.17.refs_2_
  199.6 3.3 collective-permute-done.18.refs_3_
  202.9 9.9 %collective-permute-done.20.refs_5_ = bf16[64,1536]{1,0:T(8,128)(2,1)S(1)} collective-permute-done((bf16[64,1536]{1,0:T(8,128)(2,1)}, bf16[64,1536]{1,0:T(8,128)(2,1)S(1)}, u32[]{:S(2)}, u32[]{:S(2)}) %collective-permute-start.20) | collective-permute-done | bytes 196640 | tf_op jit(solution)/shard_map/ppermute | solution.py:50
  213.6 7.6 %shard_map.311 = (bf16[64,1792]{1,0:T(8,128)(2,1)}, bf16[64,3072]{1,0:T(8,128)(2,1)}, f32[16,1536]{1,0:T(8,128)}, f32[8,1536]{1,0:T(8,128)}) custom-call(bf16[64,1536]{1,0:T(8,128)(2,1)} %get-tuple-element.117.refs_0_, bf16[64,1536]{1,0:T(8,128)(2,1)} %copy-done.37, bf16[64,1536]{1,0:T(8,128)(2,1)} %copy-done.39, bf16[64,1536]{1,0:T(8,128)(2,1)} %copy-done.42, ...), custom_call_target="tpu_custom_call" | custom-call | flops 8739999744 | bytes 27360000 | tf_op jit(solution)/shard_map/pallas_call | solution.py:714
  223.8 2.2 collective-permute-start.27
  227.5 5.5 %collective-permute-done.26.refs_5_.refs_9_ = bf16[64,1792]{1,0:T(8,128)(2,1)S(1)} collective-permute-done((bf16[64,1792]{1,0:T(8,128)(2,1)}, bf16[64,1792]{1,0:T(8,128)(2,1)S(1)}, u32[]{:S(2)}, u32[]{:S(2)}) %collective-permute-start.26) | collective-permute-done | bytes 229408 | tf_op jit(solution)/shard_map/ppermute | solution.py:46
  233.0 9.5 %collective-permute-done.27.refs_6_.refs_10_ = bf16[64,1792]{1,0:T(8,128)(2,1)S(1)} collective-permute-done((bf16[64,1792]{1,0:T(8,128)(2,1)}, bf16[64,1792]{1,0:T(8,128)(2,1)S(1)}, u32[]{:S(2)}, u32[]{:S(2)}) %collective-permute-start.27) | collective-permute-done | bytes 229408 | tf_op jit(solution)/shard_map/ppermute | solution.py:46
  243.9 8.0 %shard_map.312 = (bf16[1088,1536]{1,0:T(8,128)(2,1)}, f32[64,768]{1,0:T(8,128)}) custom-call(s32[11]{0:T(128)} %concatenate.9.flag_ref.refs_0_, bf16[1088,1536]{1,0:T(8,128)(2,1)} %convolution_convert_fusion.1.both_ref.refs_1_, bf16[64,1536]{1,0:T(8,128)(2,1)} %reshape.141.query_ref.refs_2_, f32[2,4,8,256]{3,2,1,0:T(8,128)} %get-tuple-element.104.refs_3_, ...), custom_call_target="tpu_custom_call" | custom-call | flops 9200000000 | bytes 28800000 | tf_op jit(solution)/shard_map/pallas_call | solution.py:772
  251.9 6.9 %convolution_convert_fusion.5 = bf16[768,1536]{1,0:T(8,128)(2,1)S(1)} fusion(bf16[1088,1536]{1,0:T(8,128)(2,1)} %get-tuple-element.134.refs_0_.refs_2_, bf16[192,1088]{1,0:T(8,128)(2,1)S(1)} %copy-done.12, bf16[192,1088]{1,0:T(8,128)(2,1)S(1)} %copy-done.13, bf16[192,1088]{1,0:T(8,128)(2,1)S(1)} %copy-done.14, bf16[192,1088]{1,0:T(8,128)(2,1)S(1)} %copy-done.11), kind=kOutput, calls=%fused_computation.11 | convolution fusion | flops 2574778368 | bytes 7372800 | tf_op jit(solution)/shard_map/dot_general | solution.py:29
  259.5 3.4 convolution_convert_fusion.4
  262.9 8.1 %shard_map.313 = (bf16[1088,1536]{1,0:T(8,128)(2,1)}, f32[64,768]{1,0:T(8,128)}) custom-call(s32[11]{0:T(128)} %concatenate.9.flag_ref.refs_0_, bf16[1088,1536]{1,0:T(8,128)(2,1)} %convolution_convert_fusion.both_ref.refs_1_, bf16[64,1536]{1,0:T(8,128)(2,1)} %reshape.141.query_ref.refs_2_, f32[2,4,8,256]{3,2,1,0:T(8,128)} %get-tuple-element.131.refs_3_, ...), custom_call_target="tpu_custom_call" | custom-call | flops 9200000000 | bytes 28800000 | tf_op jit(solution)/shard_map/pallas_call | solution.py:772
  271.0 2.0 fusion.3
  273.0 3.6 all-to-all-start.3
  276.9 21.8 %shard_map.314 = (bf16[1024,1536]{1,0:T(8,128)(2,1)}, f32[16,1536]{1,0:T(8,128)}, f32[64,1536]{1,0:T(8,128)}) custom-call(s32[11]{0:T(128)} %concatenate.9.flag_ref.refs_0_, bf16[1088,1536]{1,0:T(8,128)(2,1)} %get-tuple-element.134.refs_0_.refs_2_, bf16[1088,1536]{1,0:T(8,128)(2,1)} %get-tuple-element.147.refs_1_.refs_3_, ...), custom_call_target="tpu_custom_call" | custom-call | flops 24149999616 | bytes 75600000 | tf_op jit(solution)/shard_map/pallas_call | solution.py:809
  298.8 23.3 %all-to-all-done.3.refs_0_ = bf16[4,192,1536]{2,1,0:T(8,128)(2,1)S(1)} async-done(((bf16[4,192,1536]{2,1,0:T(8,128)(2,1)}), bf16[4,192,1536]{2,1,0:T(8,128)(2,1)S(1)}, u32[]{:S(2)}, u32[]{:S(2)}) %all-to-all-start.3) | async-done | bytes 2359328 | tf_op jit(solution)/shard_map/all_to_all | solution.py:748
  322.1 3.6 shard_map.315
  325.7 7.0 %convolution_convert_fusion.3 = bf16[768,1536]{1,0:T(8,128)(2,1)} fusion(bf16[1088,1536]{1,0:T(8,128)(2,1)} %get-tuple-element.147.refs_1_.refs_3_, bf16[192,1088]{1,0:T(8,128)(2,1)} %get-tuple-element.237, bf16[192,1088]{1,0:T(8,128)(2,1)} %get-tuple-element.238, bf16[192,1088]{1,0:T(8,128)(2,1)} %get-tuple-element.239, bf16[192,1088]{1,0:T(8,128)(2,1)S(1)} %copy-done.11), kind=kOutput, calls=%fused_computation.9 | convolution fusion | flops 2574778368 | bytes 7372800 | tf_op jit(solution)/shard_map/dot_general | solution.py:29
  332.7 7.1 %convolution_convert_fusion.2 = bf16[768,1536]{1,0:T(8,128)(2,1)} fusion(bf16[768,1088]{1,0:T(8,128)(2,1)} %pad_maximum_fusion.1, bf16[1088,1536]{1,0:T(8,128)(2,1)} %get-tuple-element.147.refs_1_.refs_3_), kind=kOutput, calls=%fused_computation.8 | convolution fusion | flops 2568093696 | bytes 7372800 | tf_op jit(solution)/shard_map/dot_general | solution.py:29
  339.8 3.3 convolution_bitcast_fusion.refs_1_
  343.1 2.0 fusion.2
  345.2 3.6 all-to-all-start.4
  348.9 3.8 shard_map.316
  352.7 4.7 collective-permute-start.34
  360.0 15.0 %shard_map.317 = (bf16[2048,768]{1,0:T(8,128)(2,1)}, bf16[2048,768]{1,0:T(8,128)(2,1)}) custom-call(bf16[2048,1536]{1,0:T(8,128)(2,1)} %bitcast.101, bf16[2048,1536]{1,0:T(8,128)(2,1)} %bitcast.99, bf16[1536,768]{1,0:T(8,128)(2,1)} %bitcast.87, bf16[768,1536]{1,0:T(8,128)(2,1)} %down_ref.1), custom_call_target="tpu_custom_call" | custom-call | flops 17250000896 | bytes 54000000 | tf_op jit(solution)/shard_map/pallas_call | solution.py:872
  375.0 3.9 collective-permute-done.35
  378.9 2.0 add_convert_fusion.refs_0_
  382.3 3.1 shard_map.318
  385.4 6.8 %collective-permute-start.31 = (bf16[48,1536]{1,0:T(8,128)(2,1)}, bf16[48,1536]{1,0:T(8,128)(2,1)S(1)}, u32[]{:S(2)}, u32[]{:S(2)}) collective-permute-start(bf16[48,1536]{1,0:T(8,128)(2,1)} %get-tuple-element.163), channel_id=1, source_target_pairs={{0,1},{1,2},{2,3},{3,0},{4,5},{5,6},{6,7},{7,4},{8,9},{9,10},{10,1... | collective-permute-start | bytes 442376 | tf_op jit(solution)/shard_map/ppermute | solution.py:46
  394.5 9.2 %shard_map.319 = bf16[1536,768]{1,0:T(8,128)(2,1)} custom-call(bf16[2048,1536]{1,0:T(8,128)(2,1)} %bitcast.102, bf16[2048,768]{1,0:T(8,128)(2,1)} %get-tuple-element.167.right_ref), custom_call_target="tpu_custom_call" | custom-call | flops 10924999680 | bytes 34200000 | tf_op jit(solution)/shard_map/pallas_call | solution.py:885
  405.6 3.2 collective-permute-start.37
  408.8 1.8 collective-permute-start.38
  413.7 3.6 all-to-all-start.5
  418.9 8.9 %collective-permute-done.38 = bf16[24,1536]{1,0:T(8,128)(2,1)} collective-permute-done((bf16[24,1536]{1,0:T(8,128)(2,1)}, bf16[24,1536]{1,0:T(8,128)(2,1)}, u32[]{:S(2)}, u32[]{:S(2)}) %collective-permute-start.38) | collective-permute-done | bytes 73760 | tf_op jit(solution)/shard_map/ppermute | solution.py:46
  431.0 2.9 collective-permute-start.40
  433.9 2.4 collective-permute-start.42
  436.3 6.5 %collective-permute-done.51.refs_2_ = bf16[48,3072]{1,0:T(8,128)(2,1)} collective-permute-done((bf16[48,3072]{1,0:T(8,128)(2,1)S(1)}, bf16[48,3072]{1,0:T(8,128)(2,1)}, u32[]{:S(2)}, u32[]{:S(2)}) %collective-permute-start.51) | collective-permute-done | bytes 294944 | tf_op jit(solution)/shard_map/ppermute | solution.py:46
  442.8 9.8 %shard_map.322 = f32[768,1536]{1,0:T(8,128)} custom-call(bf16[2048,768]{1,0:T(8,128)(2,1)} %get-tuple-element.176.left_ref, bf16[2048,1536]{1,0:T(8,128)(2,1)} %bitcast.100), custom_call_target="tpu_custom_call" | custom-call | flops 10924999680 | bytes 34200000 | tf_op jit(solution)/shard_map/pallas_call | solution.py:885
  453.9 3.4 shard_map.321
  459.3 2.7 convert_element_type.130
  462.1 12.4 %all-gather.15.cloned.1.call-done.refs_10_ = f32[192,1536]{1,0:T(8,128)} async-done(((f32[24,1536]{1,0:T(8,128)}), f32[192,1536]{1,0:T(8,128)}) %all-gather.15.cloned.1.call-update) | async-done | bytes 1179664 | tf_op jit(solution)/shard_map/all_gather | solution.py:916
  479.3 2.4 fusion.7
  487.8 2.9 shard_map.320
  (275 shorter events, 74.9 us)
Async XLA Ops:
  7.2 80.0 %all-gather.9.cloned.1.call-start = ((), (), s32[]{:S(2)}) async-start(), calls=%async_computation.8 | async-start | bytes 12386304 | tf_op jit(solution)/shard_map/all_gather | solution.py:574
  10.0 128.3 %all-gather.11.cloned.1.call-start = ((), (), s32[]{:S(2)}) async-start(), calls=%async_computation.9 | async-start | bytes 5308416 | tf_op jit(solution)/shard_map/all_gather | solution.py:623
  26.1 21.6 %all-to-all-start = ((f32[8,64,192]{2,1,0:T(8,128)}), f32[8,64,192]{2,1,0:T(8,128)S(1)}, u32[]{:S(2)}, u32[]{:S(2)}) async-start(f32[8,64,192]{2,1,0:T(8,128)} %bitcast.76), calls=%async_computation | async-start | bytes 1048576 | tf_op jit(solution)/shard_map/all_to_all | solution.py:564
  31.3 21.3 %collective-permute-start.23 = (bf16[64,1536]{1,0:T(8,128)(2,1)S(1)}, bf16[64,1536]{1,0:T(8,128)(2,1)}, u32[]{:S(2)}, u32[]{:S(2)}) collective-permute-start(bf16[64,1536]{1,0:T(8,128)(2,1)S(1)} %copy-done.20), channel_id=1, source_target_pairs={{0,1},{1,2},{2,3},{3,0},{4,5},{5,6},{6,7},{7,4},{8,9},{9,10},{10,1... | collective-permute-start | bytes 589832 | tf_op jit(solution)/shard_map/ppermute | solution.py:46
  32.9 19.7 %collective-permute-start.24 = (bf16[64,1536]{1,0:T(8,128)(2,1)S(1)}, bf16[64,1536]{1,0:T(8,128)(2,1)}, u32[]{:S(2)}, u32[]{:S(2)}) collective-permute-start(bf16[64,1536]{1,0:T(8,128)(2,1)S(1)} %copy-done.20), channel_id=1, source_target_pairs={{0,2},{1,3},{2,0},{3,1},{4,6},{5,7},{6,4},{7,5},{8,10},{9,11},{10,... | collective-permute-start | bytes 589832 | tf_op jit(solution)/shard_map/ppermute | solution.py:46
  35.5 17.1 %collective-permute-start.25 = (bf16[64,1536]{1,0:T(8,128)(2,1)S(1)}, bf16[64,1536]{1,0:T(8,128)(2,1)}, u32[]{:S(2)}, u32[]{:S(2)}) collective-permute-start(bf16[64,1536]{1,0:T(8,128)(2,1)S(1)} %copy-done.20), channel_id=1, source_target_pairs={{0,3},{1,0},{2,1},{3,2},{4,7},{5,4},{6,5},{7,6},{8,11},{9,8},{10,9... | collective-permute-start | bytes 589832 | tf_op jit(solution)/shard_map/ppermute | solution.py:46
  48.5 14.2 %all-to-all-start.1 = ((bf16[8,64,192]{2,1,0:T(8,128)(2,1)}), bf16[8,64,192]{2,1,0:T(8,128)(2,1)S(1)}, u32[]{:S(2)}, u32[]{:S(2)}) async-start(bf16[8,64,192]{2,1,0:T(8,128)(2,1)} %broadcast_in_dim.51), calls=%async_computation.1 | async-start | bytes 524288 | tf_op jit(solution)/shard_map/all_to_all | solution.py:582
  52.6 174.9 %all-gather.19.cloned.1.call-start = ((), (), s32[]{:S(2)}) async-start(), calls=%async_computation.15 | async-start | bytes 7077888 | tf_op jit(solution)/shard_map/all_gather | solution.py:675
  123.1 57.2 %all-to-all-start.2 = ((bf16[192,8,768]{2,0,1:T(8,128)(2,1)}), bf16[192,8,768]{2,0,1:T(8,128)(2,1)S(1)}, u32[]{:S(2)}, u32[]{:S(2)}) async-start(bf16[192,8,768]{2,0,1:T(8,128)(2,1)} %bitcast.75), calls=%async_computation.2 | async-start | bytes 4718592 | tf_op jit(solution)/shard_map/all_to_all | solution.py:674
  127.3 205.4 %all-gather.13.cloned.1.call-start = ((), (), s32[]{:S(2)}) async-start(), calls=%async_computation.10 | async-start | bytes 3538944 | tf_op jit(solution)/shard_map/all_gather | solution.py:726
  127.4 7.7 %collective-permute-start.3 = (bf16[64,896]{1,0:T(8,128)(2,1)}, bf16[64,896]{1,0:T(8,128)(2,1)}, u32[]{:S(2)}, u32[]{:S(2)}) collective-permute-start(bf16[64,896]{1,0:T(8,128)(2,1)} %get-tuple-element.107), channel_id=1, source_target_pairs={{0,1},{1,2},{2,3},{3,0},{4,5},{5,6},{6,7},{7,4},{8,9},{9,10},{10,1... | collective-permute-start | bytes 344072 | tf_op jit(solution)/shard_map/ppermute | solution.py:46
  130.0 14.2 %collective-permute-start.4 = (bf16[64,896]{1,0:T(8,128)(2,1)}, bf16[64,896]{1,0:T(8,128)(2,1)}, u32[]{:S(2)}, u32[]{:S(2)}) collective-permute-start(bf16[64,896]{1,0:T(8,128)(2,1)} %get-tuple-element.108), channel_id=1, source_target_pairs={{0,2},{1,3},{2,0},{3,1},{4,6},{5,7},{6,4},{7,5},{8,10},{9,11},{10,... | collective-permute-start | bytes 344072 | tf_op jit(solution)/shard_map/ppermute | solution.py:46
  132.5 11.7 %collective-permute-start.5 = (bf16[64,896]{1,0:T(8,128)(2,1)}, bf16[64,896]{1,0:T(8,128)(2,1)}, u32[]{:S(2)}, u32[]{:S(2)}) collective-permute-start(bf16[64,896]{1,0:T(8,128)(2,1)} %get-tuple-element.109), channel_id=1, source_target_pairs={{0,3},{1,0},{2,1},{3,2},{4,7},{5,4},{6,5},{7,6},{8,11},{9,8},{10,9... | collective-permute-start | bytes 344072 | tf_op jit(solution)/shard_map/ppermute | solution.py:46
  133.8 10.3 %collective-permute-start = (bf16[64,896]{1,0:T(8,128)(2,1)}, bf16[64,896]{1,0:T(8,128)(2,1)}, u32[]{:S(2)}, u32[]{:S(2)}) collective-permute-start(bf16[64,896]{1,0:T(8,128)(2,1)} %get-tuple-element.101), channel_id=1, source_target_pairs={{0,1},{1,2},{2,3},{3,0},{4,5},{5,6},{6,7},{7,4},{8,9},{9,10},{10,1... | collective-permute-start | bytes 344072 | tf_op jit(solution)/shard_map/ppermute | solution.py:46
  134.5 15.3 %collective-permute-start.1 = (bf16[64,896]{1,0:T(8,128)(2,1)}, bf16[64,896]{1,0:T(8,128)(2,1)}, u32[]{:S(2)}, u32[]{:S(2)}) collective-permute-start(bf16[64,896]{1,0:T(8,128)(2,1)} %get-tuple-element.102), channel_id=1, source_target_pairs={{0,2},{1,3},{2,0},{3,1},{4,6},{5,7},{6,4},{7,5},{8,10},{9,11},{10,... | collective-permute-start | bytes 344072 | tf_op jit(solution)/shard_map/ppermute | solution.py:46
  135.1 14.7 %collective-permute-start.2 = (bf16[64,896]{1,0:T(8,128)(2,1)S(1)}, bf16[64,896]{1,0:T(8,128)(2,1)}, u32[]{:S(2)}, u32[]{:S(2)}) collective-permute-start(bf16[64,896]{1,0:T(8,128)(2,1)S(1)} %copy-done.53), channel_id=1, source_target_pairs={{0,3},{1,0},{2,1},{3,2},{4,7},{5,4},{6,5},{7,6},{8,11},{9,8},{10,9... | collective-permute-start | bytes 344072 | tf_op jit(solution)/shard_map/ppermute | solution.py:46
  156.0 17.3 %collective-permute-start.9 = (bf16[64,1536]{1,0:T(8,128)(2,1)}, bf16[64,1536]{1,0:T(8,128)(2,1)S(1)}, u32[]{:S(2)}, u32[]{:S(2)}) collective-permute-start(bf16[64,1536]{1,0:T(8,128)(2,1)} %get-tuple-element.115.refs_0_), channel_id=1, source_target_pairs={{0,16},{4,20},{8,24},{12,28},{16,0},{20,4},{24,8},{28,12},{1,17},{... | collective-permute-start | bytes 589832 | tf_op jit(solution)/shard_map/ppermute | solution.py:50
  157.7 15.6 %collective-permute-start.11 = (bf16[64,1536]{1,0:T(8,128)(2,1)}, bf16[64,1536]{1,0:T(8,128)(2,1)S(1)}, u32[]{:S(2)}, u32[]{:S(2)}) collective-permute-start(bf16[64,1536]{1,0:T(8,128)(2,1)} %get-tuple-element.115.refs_0_), channel_id=1, source_target_pairs={{0,24},{4,28},{8,16},{12,20},{16,8},{20,12},{24,0},{28,4},{1,25},{... | collective-permute-start | bytes 589832 | tf_op jit(solution)/shard_map/ppermute | solution.py:50
  159.2 14.6 %collective-permute-start.7 = (bf16[64,1536]{1,0:T(8,128)(2,1)}, bf16[64,1536]{1,0:T(8,128)(2,1)S(1)}, u32[]{:S(2)}, u32[]{:S(2)}) collective-permute-start(bf16[64,1536]{1,0:T(8,128)(2,1)} %get-tuple-element.115.refs_0_), channel_id=1, source_target_pairs={{0,8},{4,12},{8,0},{12,4},{16,24},{20,28},{24,16},{28,20},{1,9},{5... | collective-permute-start | bytes 589832 | tf_op jit(solution)/shard_map/ppermute | solution.py:50
  159.5 14.4 %collective-permute-start.6 = (bf16[64,1536]{1,0:T(8,128)(2,1)}, bf16[64,1536]{1,0:T(8,128)(2,1)S(1)}, u32[]{:S(2)}, u32[]{:S(2)}) collective-permute-start(bf16[64,1536]{1,0:T(8,128)(2,1)} %get-tuple-element.115.refs_0_), channel_id=1, source_target_pairs={{0,4},{4,0},{8,12},{12,8},{16,20},{20,16},{24,28},{28,24},{1,5},{5... | collective-permute-start | bytes 589832 | tf_op jit(solution)/shard_map/ppermute | solution.py:50
  173.3 2.2 collective-permute-start.12
  173.8 2.3 collective-permute-start.8
  176.1 16.7 %collective-permute-start.13 = (bf16[64,1536]{1,0:T(8,128)(2,1)}, bf16[64,1536]{1,0:T(8,128)(2,1)S(1)}, u32[]{:S(2)}, u32[]{:S(2)}) collective-permute-start(bf16[64,1536]{1,0:T(8,128)(2,1)} %get-tuple-element.115.refs_0_), channel_id=1, source_target_pairs={{0,1},{1,2},{2,3},{3,0},{4,5},{5,6},{6,7},{7,4},{8,9},{9,10},{10,1... | collective-permute-start | bytes 589832 | tf_op jit(solution)/shard_map/ppermute | solution.py:46
  177.5 16.1 %collective-permute-start.14 = (bf16[64,1536]{1,0:T(8,128)(2,1)}, bf16[64,1536]{1,0:T(8,128)(2,1)S(1)}, u32[]{:S(2)}, u32[]{:S(2)}) collective-permute-start(bf16[64,1536]{1,0:T(8,128)(2,1)} %get-tuple-element.115.refs_0_), channel_id=1, source_target_pairs={{0,2},{1,3},{2,0},{3,1},{4,6},{5,7},{6,4},{7,5},{8,10},{9,11},{10,... | collective-permute-start | bytes 589832 | tf_op jit(solution)/shard_map/ppermute | solution.py:46
  179.3 15.3 %collective-permute-start.15 = (bf16[64,1536]{1,0:T(8,128)(2,1)}, bf16[64,1536]{1,0:T(8,128)(2,1)S(1)}, u32[]{:S(2)}, u32[]{:S(2)}) collective-permute-start(bf16[64,1536]{1,0:T(8,128)(2,1)} %get-tuple-element.115.refs_0_), channel_id=1, source_target_pairs={{0,3},{1,0},{2,1},{3,2},{4,7},{5,4},{6,5},{7,6},{8,11},{9,8},{10,9... | collective-permute-start | bytes 589832 | tf_op jit(solution)/shard_map/ppermute | solution.py:46
  191.5 3.7 collective-permute-start.16
  191.6 8.0 %collective-permute-start.17 = (bf16[64,1536]{1,0:T(8,128)(2,1)}, bf16[64,1536]{1,0:T(8,128)(2,1)S(1)}, u32[]{:S(2)}, u32[]{:S(2)}) collective-permute-start(bf16[64,1536]{1,0:T(8,128)(2,1)} %get-tuple-element.119), channel_id=1, source_target_pairs={{0,8},{4,12},{8,0},{12,4},{16,24},{20,28},{24,16},{28,20},{1,9},{5... | collective-permute-start | bytes 589832 | tf_op jit(solution)/shard_map/ppermute | solution.py:50
  192.8 10.1 %collective-permute-start.18 = (bf16[64,1536]{1,0:T(8,128)(2,1)}, bf16[64,1536]{1,0:T(8,128)(2,1)S(1)}, u32[]{:S(2)}, u32[]{:S(2)}) collective-permute-start(bf16[64,1536]{1,0:T(8,128)(2,1)} %get-tuple-element.120), channel_id=1, source_target_pairs={{0,12},{4,8},{8,4},{12,0},{16,28},{20,24},{24,20},{28,16},{1,13},{... | collective-permute-start | bytes 589832 | tf_op jit(solution)/shard_map/ppermute | solution.py:50
  193.6 9.3 %collective-permute-start.19 = (bf16[64,1536]{1,0:T(8,128)(2,1)}, bf16[64,1536]{1,0:T(8,128)(2,1)S(1)}, u32[]{:S(2)}, u32[]{:S(2)}) collective-permute-start(bf16[64,1536]{1,0:T(8,128)(2,1)} %get-tuple-element.121), channel_id=1, source_target_pairs={{0,16},{4,20},{8,24},{12,28},{16,0},{20,4},{24,8},{28,12},{1,17},{... | collective-permute-start | bytes 589832 | tf_op jit(solution)/shard_map/ppermute | solution.py:50
  194.6 18.2 %collective-permute-start.20 = (bf16[64,1536]{1,0:T(8,128)(2,1)}, bf16[64,1536]{1,0:T(8,128)(2,1)S(1)}, u32[]{:S(2)}, u32[]{:S(2)}) collective-permute-start(bf16[64,1536]{1,0:T(8,128)(2,1)} %get-tuple-element.122), channel_id=1, source_target_pairs={{0,20},{4,16},{8,28},{12,24},{16,4},{20,0},{24,12},{28,8},{1,21},{... | collective-permute-start | bytes 589832 | tf_op jit(solution)/shard_map/ppermute | solution.py:50
  195.2 17.6 %collective-permute-start.21 = (bf16[64,1536]{1,0:T(8,128)(2,1)}, bf16[64,1536]{1,0:T(8,128)(2,1)S(1)}, u32[]{:S(2)}, u32[]{:S(2)}) collective-permute-start(bf16[64,1536]{1,0:T(8,128)(2,1)} %get-tuple-element.123), channel_id=1, source_target_pairs={{0,24},{4,28},{8,16},{12,20},{16,8},{20,12},{24,0},{28,4},{1,25},{... | collective-permute-start | bytes 589832 | tf_op jit(solution)/shard_map/ppermute | solution.py:50
  199.6 13.2 %collective-permute-start.22 = (bf16[64,1536]{1,0:T(8,128)(2,1)}, bf16[64,1536]{1,0:T(8,128)(2,1)S(1)}, u32[]{:S(2)}, u32[]{:S(2)}) collective-permute-start(bf16[64,1536]{1,0:T(8,128)(2,1)} %get-tuple-element.124), channel_id=1, source_target_pairs={{0,28},{4,24},{8,20},{12,16},{16,12},{20,8},{24,4},{28,0},{1,29},{... | collective-permute-start | bytes 589832 | tf_op jit(solution)/shard_map/ppermute | solution.py:50
  221.3 138.7 %all-gather.17.cloned.1.call-start = ((), (), s32[]{:S(2)}) async-start(), calls=%async_computation.14 | async-start | bytes 7077888 | tf_op jit(solution)/shard_map/all_gather | solution.py:727
  222.3 10.7 %collective-permute-start.26 = (bf16[64,1792]{1,0:T(8,128)(2,1)}, bf16[64,1792]{1,0:T(8,128)(2,1)S(1)}, u32[]{:S(2)}, u32[]{:S(2)}) collective-permute-start(bf16[64,1792]{1,0:T(8,128)(2,1)} %get-tuple-element.133.refs_4_.refs_8_), channel_id=1, source_target_pairs={{0,1},{1,2},{2,3},{3,0},{4,5},{5,6},{6,7},{7,4},{8,9},{9,10},{10,1... | collective-permute-start | bytes 688136 | tf_op jit(solution)/shard_map/ppermute | solution.py:46
  223.8 18.7 %collective-permute-start.27 = (bf16[64,1792]{1,0:T(8,128)(2,1)}, bf16[64,1792]{1,0:T(8,128)(2,1)S(1)}, u32[]{:S(2)}, u32[]{:S(2)}) collective-permute-start(bf16[64,1792]{1,0:T(8,128)(2,1)} %get-tuple-element.133.refs_4_.refs_8_), channel_id=1, source_target_pairs={{0,2},{1,3},{2,0},{3,1},{4,6},{5,7},{6,4},{7,5},{8,10},{9,11},{10,... | collective-permute-start | bytes 688136 | tf_op jit(solution)/shard_map/ppermute | solution.py:46
  226.1 16.4 %collective-permute-start.28 = (bf16[64,1792]{1,0:T(8,128)(2,1)}, bf16[64,1792]{1,0:T(8,128)(2,1)S(1)}, u32[]{:S(2)}, u32[]{:S(2)}) collective-permute-start(bf16[64,1792]{1,0:T(8,128)(2,1)} %get-tuple-element.133.refs_4_.refs_8_), channel_id=1, source_target_pairs={{0,3},{1,0},{2,1},{3,2},{4,7},{5,4},{6,5},{7,6},{8,11},{9,8},{10,9... | collective-permute-start | bytes 688136 | tf_op jit(solution)/shard_map/ppermute | solution.py:46
  258.8 12.2 %collective-permute-start.29 = (bf16[768,1536]{1,0:T(8,128)(2,1)S(1)}, bf16[768,1536]{1,0:T(8,128)(2,1)S(1)}, u32[]{:S(2)}, u32[]{:S(2)}) collective-permute-start(bf16[768,1536]{1,0:T(8,128)(2,1)S(1)} %convolution_convert_fusion.5), channel_id=1, source_target_pairs={{0,4},{4,0},{8,12},{12,8},{16,20},{20,16},{24,28},{28,24},{1,5},{5... | collective-permute-start | bytes 7077896 | tf_op jit(solution)/shard_map/ppermute | solution.py:50
  273.0 49.0 %all-to-all-start.3 = ((bf16[4,192,1536]{2,1,0:T(8,128)(2,1)}), bf16[4,192,1536]{2,1,0:T(8,128)(2,1)S(1)}, u32[]{:S(2)}, u32[]{:S(2)}) async-start(bf16[4,192,1536]{2,1,0:T(8,128)(2,1)} %fusion.3), calls=%async_computation.3 | async-start | bytes 4718592 | tf_op jit(solution)/shard_map/all_to_all | solution.py:748
  276.7 127.2 %reduce-scatter.5.cloned.1.call-start = ((), (), s32[]{:S(2)}) async-start(), calls=%async_computation.12 | async-start | bytes 1327104 | tf_op jit(solution)/shard_map/reduce_scatter | solution.py:859
  332.7 10.4 %collective-permute-start.30 = (bf16[768,1536]{1,0:T(8,128)(2,1)}, bf16[768,1536]{1,0:T(8,128)(2,1)S(1)}, u32[]{:S(2)}, u32[]{:S(2)}) collective-permute-start(bf16[768,1536]{1,0:T(8,128)(2,1)} %convolution_convert_fusion.3), channel_id=1, source_target_pairs={{0,4},{4,0},{8,12},{12,8},{16,20},{20,16},{24,28},{28,24},{1,5},{5... | collective-permute-start | bytes 7077896 | tf_op jit(solution)/shard_map/ppermute | solution.py:50
  345.2 35.7 %all-to-all-start.4 = ((bf16[4,192,1536]{2,1,0:T(8,128)(2,1)}), bf16[4,192,1536]{2,1,0:T(8,128)(2,1)S(1)}, u32[]{:S(2)}, u32[]{:S(2)}) async-start(bf16[4,192,1536]{2,1,0:T(8,128)(2,1)} %fusion.2), calls=%async_computation.6 | async-start | bytes 4718592 | tf_op jit(solution)/shard_map/all_to_all | solution.py:748
  348.8 108.5 %reduce-scatter.3.cloned.1.call-start = ((), (), s32[]{:S(2)}) async-start(), calls=%async_computation.11 | async-start | bytes 1769472 | tf_op jit(solution)/shard_map/reduce_scatter | solution.py:900
  352.7 22.3 %collective-permute-start.34 = (bf16[48,3072]{1,0:T(8,128)(2,1)}, bf16[48,3072]{1,0:T(8,128)(2,1)}, u32[]{:S(2)}, u32[]{:S(2)}) collective-permute-start(bf16[48,3072]{1,0:T(8,128)(2,1)} %get-tuple-element.153), channel_id=1, source_target_pairs={{0,1},{1,2},{2,3},{3,0},{4,5},{5,6},{6,7},{7,4},{8,9},{9,10},{10,1... | collective-permute-start | bytes 884744 | tf_op jit(solution)/shard_map/ppermute | solution.py:46
  357.4 21.5 %collective-permute-start.35 = (bf16[48,3072]{1,0:T(8,128)(2,1)}, bf16[48,3072]{1,0:T(8,128)(2,1)}, u32[]{:S(2)}, u32[]{:S(2)}) collective-permute-start(bf16[48,3072]{1,0:T(8,128)(2,1)} %get-tuple-element.154), channel_id=1, source_target_pairs={{0,2},{1,3},{2,0},{3,1},{4,6},{5,7},{6,4},{7,5},{8,10},{9,11},{10,... | collective-permute-start | bytes 884744 | tf_op jit(solution)/shard_map/ppermute | solution.py:46
  358.7 20.2 %collective-permute-start.36 = (bf16[48,3072]{1,0:T(8,128)(2,1)}, bf16[48,3072]{1,0:T(8,128)(2,1)}, u32[]{:S(2)}, u32[]{:S(2)}) collective-permute-start(bf16[48,3072]{1,0:T(8,128)(2,1)} %get-tuple-element.155), channel_id=1, source_target_pairs={{0,3},{1,0},{2,1},{3,2},{4,7},{5,4},{6,5},{7,6},{8,11},{9,8},{10,9... | collective-permute-start | bytes 884744 | tf_op jit(solution)/shard_map/ppermute | solution.py:46
  385.4 18.4 %collective-permute-start.31 = (bf16[48,1536]{1,0:T(8,128)(2,1)}, bf16[48,1536]{1,0:T(8,128)(2,1)S(1)}, u32[]{:S(2)}, u32[]{:S(2)}) collective-permute-start(bf16[48,1536]{1,0:T(8,128)(2,1)} %get-tuple-element.163), channel_id=1, source_target_pairs={{0,1},{1,2},{2,3},{3,0},{4,5},{5,6},{6,7},{7,4},{8,9},{9,10},{10,1... | collective-permute-start | bytes 442376 | tf_op jit(solution)/shard_map/ppermute | solution.py:46
  392.2 11.6 %collective-permute-start.32 = (bf16[48,1536]{1,0:T(8,128)(2,1)}, bf16[48,1536]{1,0:T(8,128)(2,1)S(1)}, u32[]{:S(2)}, u32[]{:S(2)}) collective-permute-start(bf16[48,1536]{1,0:T(8,128)(2,1)} %get-tuple-element.164), channel_id=1, source_target_pairs={{0,2},{1,3},{2,0},{3,1},{4,6},{5,7},{6,4},{7,5},{8,10},{9,11},{10,... | collective-permute-start | bytes 442376 | tf_op jit(solution)/shard_map/ppermute | solution.py:46
  393.5 10.2 %collective-permute-start.33 = (bf16[48,1536]{1,0:T(8,128)(2,1)}, bf16[48,1536]{1,0:T(8,128)(2,1)S(1)}, u32[]{:S(2)}, u32[]{:S(2)}) collective-permute-start(bf16[48,1536]{1,0:T(8,128)(2,1)} %get-tuple-element.165), channel_id=1, source_target_pairs={{0,3},{1,0},{2,1},{3,2},{4,7},{5,4},{6,5},{7,6},{8,11},{9,8},{10,9... | collective-permute-start | bytes 442376 | tf_op jit(solution)/shard_map/ppermute | solution.py:46
  405.6 11.9 %collective-permute-start.37 = (bf16[24,1536]{1,0:T(8,128)(2,1)}, bf16[24,1536]{1,0:T(8,128)(2,1)}, u32[]{:S(2)}, u32[]{:S(2)}) collective-permute-start(bf16[24,1536]{1,0:T(8,128)(2,1)} %convert_element_type.126), channel_id=1, source_target_pairs={{0,1},{1,2},{2,3},{3,0},{4,5},{5,6},{6,7},{7,4},{8,9},{9,10},{10,1... | collective-permute-start | bytes 221192 | tf_op jit(solution)/shard_map/ppermute | solution.py:46
  408.8 19.0 %collective-permute-start.38 = (bf16[24,1536]{1,0:T(8,128)(2,1)}, bf16[24,1536]{1,0:T(8,128)(2,1)}, u32[]{:S(2)}, u32[]{:S(2)}) collective-permute-start(bf16[24,1536]{1,0:T(8,128)(2,1)} %convert_element_type.126), channel_id=1, source_target_pairs={{0,2},{1,3},{2,0},{3,1},{4,6},{5,7},{6,4},{7,5},{8,10},{9,11},{10,... | collective-permute-start | bytes 221192 | tf_op jit(solution)/shard_map/ppermute | solution.py:46
  410.6 17.3 %collective-permute-start.39 = (bf16[24,1536]{1,0:T(8,128)(2,1)}, bf16[24,1536]{1,0:T(8,128)(2,1)}, u32[]{:S(2)}, u32[]{:S(2)}) collective-permute-start(bf16[24,1536]{1,0:T(8,128)(2,1)} %convert_element_type.126), channel_id=1, source_target_pairs={{0,3},{1,0},{2,1},{3,2},{4,7},{5,4},{6,5},{7,6},{8,11},{9,8},{10,9... | collective-permute-start | bytes 221192 | tf_op jit(solution)/shard_map/ppermute | solution.py:46
  411.2 22.8 %collective-permute-start.50 = (bf16[48,3072]{1,0:T(8,128)(2,1)S(1)}, bf16[48,3072]{1,0:T(8,128)(2,1)}, u32[]{:S(2)}, u32[]{:S(2)}) collective-permute-start(bf16[48,3072]{1,0:T(8,128)(2,1)S(1)} %copy-done.17), channel_id=1, source_target_pairs={{0,1},{1,2},{2,3},{3,0},{4,5},{5,6},{6,7},{7,4},{8,9},{9,10},{10,1... | collective-permute-start | bytes 884744 | tf_op jit(solution)/shard_map/ppermute | solution.py:46
  412.6 30.2 %collective-permute-start.51 = (bf16[48,3072]{1,0:T(8,128)(2,1)S(1)}, bf16[48,3072]{1,0:T(8,128)(2,1)}, u32[]{:S(2)}, u32[]{:S(2)}) collective-permute-start(bf16[48,3072]{1,0:T(8,128)(2,1)S(1)} %copy-done.17), channel_id=1, source_target_pairs={{0,2},{1,3},{2,0},{3,1},{4,6},{5,7},{6,4},{7,5},{8,10},{9,11},{10,... | collective-permute-start | bytes 884744 | tf_op jit(solution)/shard_map/ppermute | solution.py:46
  413.7 45.3 %all-to-all-start.5 = ((bf16[8,192,768]{2,1,0:T(8,128)(2,1)}), bf16[8,192,768]{2,1,0:T(8,128)(2,1)S(1)}, u32[]{:S(2)}, u32[]{:S(2)}) async-start(bf16[8,192,768]{2,1,0:T(8,128)(2,1)} %bitcast.88), calls=%async_computation.7 | async-start | bytes 4718592 | tf_op jit(solution)/shard_map/all_to_all | solution.py:903
  417.4 57.1 %all-gather.15.cloned.1.call-start = ((), (), s32[]{:S(2)}) async-start(), calls=%async_computation.13 | async-start | bytes 1327104 | tf_op jit(solution)/shard_map/all_gather | solution.py:916
  417.4 25.4 %collective-permute-start.52 = (bf16[48,3072]{1,0:T(8,128)(2,1)S(1)}, bf16[48,3072]{1,0:T(8,128)(2,1)}, u32[]{:S(2)}, u32[]{:S(2)}) collective-permute-start(bf16[48,3072]{1,0:T(8,128)(2,1)S(1)} %copy-done.17), channel_id=1, source_target_pairs={{0,3},{1,0},{2,1},{3,2},{4,7},{5,4},{6,5},{7,6},{8,11},{9,8},{10,9... | collective-permute-start | bytes 884744 | tf_op jit(solution)/shard_map/ppermute | solution.py:46
  431.0 21.5 %collective-permute-start.40 = (bf16[48,1536]{1,0:T(8,128)(2,1)S(1)}, bf16[48,1536]{1,0:T(8,128)(2,1)S(1)}, u32[]{:S(2)}, u32[]{:S(2)}) collective-permute-start(bf16[48,1536]{1,0:T(8,128)(2,1)S(1)} %add_convert_fusion.2.refs_4_), channel_id=1, source_target_pairs={{0,1},{1,2},{2,3},{3,0},{4,5},{5,6},{6,7},{7,4},{8,9},{9,10},{10,1... | collective-permute-start | bytes 442376 | tf_op jit(solution)/shard_map/ppermute | solution.py:46
  433.9 18.7 %collective-permute-start.41 = (bf16[48,1536]{1,0:T(8,128)(2,1)S(1)}, bf16[48,1536]{1,0:T(8,128)(2,1)S(1)}, u32[]{:S(2)}, u32[]{:S(2)}) collective-permute-start(bf16[48,1536]{1,0:T(8,128)(2,1)S(1)} %add_convert_fusion.2.refs_4_), channel_id=1, source_target_pairs={{0,2},{1,3},{2,0},{3,1},{4,6},{5,7},{6,4},{7,5},{8,10},{9,11},{10,... | collective-permute-start | bytes 442376 | tf_op jit(solution)/shard_map/ppermute | solution.py:46
  433.9 18.7 %collective-permute-start.42 = (bf16[48,1536]{1,0:T(8,128)(2,1)S(1)}, bf16[48,1536]{1,0:T(8,128)(2,1)S(1)}, u32[]{:S(2)}, u32[]{:S(2)}) collective-permute-start(bf16[48,1536]{1,0:T(8,128)(2,1)S(1)} %add_convert_fusion.2.refs_4_), channel_id=1, source_target_pairs={{0,3},{1,0},{2,1},{3,2},{4,7},{5,4},{6,5},{7,6},{8,11},{9,8},{10,9... | collective-permute-start | bytes 442376 | tf_op jit(solution)/shard_map/ppermute | solution.py:46
  475.7 9.1 %collective-permute-start.44 = (f32[64,192]{1,0:T(8,128)S(1)}, f32[64,192]{1,0:T(8,128)S(1)}, u32[]{:S(2)}, u32[]{:S(2)}) collective-permute-start(f32[64,192]{1,0:T(8,128)S(1)} %fusion.6.refs_0_), channel_id=1, source_target_pairs={{0,8},{4,12},{8,0},{12,4},{16,24},{20,28},{24,16},{28,20},{1,9},{5... | collective-permute-start | bytes 147464 | tf_op jit(solution)/shard_map/ppermute | solution.py:50
  477.3 8.1 %collective-permute-start.46 = (f32[64,192]{1,0:T(8,128)S(1)}, f32[64,192]{1,0:T(8,128)S(1)}, u32[]{:S(2)}, u32[]{:S(2)}) collective-permute-start(f32[64,192]{1,0:T(8,128)S(1)} %fusion.6.refs_0_), channel_id=1, source_target_pairs={{0,16},{4,20},{8,24},{12,28},{16,0},{20,4},{24,8},{28,12},{1,17},{... | collective-permute-start | bytes 147464 | tf_op jit(solution)/shard_map/ppermute | solution.py:50
  477.8 7.6 %collective-permute-start.48 = (f32[64,192]{1,0:T(8,128)S(1)}, f32[64,192]{1,0:T(8,128)S(1)}, u32[]{:S(2)}, u32[]{:S(2)}) collective-permute-start(f32[64,192]{1,0:T(8,128)S(1)} %fusion.6.refs_0_), channel_id=1, source_target_pairs={{0,24},{4,28},{8,16},{12,20},{16,8},{20,12},{24,0},{28,4},{1,25},{... | collective-permute-start | bytes 147464 | tf_op jit(solution)/shard_map/ppermute | solution.py:50
  479.3 7.2 %collective-permute-start.43 = (f32[64,192]{1,0:T(8,128)S(1)}, f32[64,192]{1,0:T(8,128)S(1)}, u32[]{:S(2)}, u32[]{:S(2)}) collective-permute-start(f32[64,192]{1,0:T(8,128)S(1)} %fusion.6.refs_0_), channel_id=1, source_target_pairs={{0,4},{4,0},{8,12},{12,8},{16,20},{20,16},{24,28},{28,24},{1,5},{5... | collective-permute-start | bytes 147464 | tf_op jit(solution)/shard_map/ppermute | solution.py:50
  484.8 1.7 collective-permute-start.45
  (66 other events, 485.1 us)
Sparse Core Ops, SparseCore 0:
  10.5 76.6 all-gather.8
  89.0 38.9 all-gather.10
  130.5 64.5 all-gather.18
  221.4 32.4 all-gather.12
  256.2 67.6 all-gather.16
  339.9 53.7 reduce-scatter.4
  397.4 50.1 reduce-scatter.2
  450.2 24.1 all-gather.14
